TPU v7x, 128 devices: a whole 4x4x4 slice. The times are simulated.
128 devices in a mesh: row: 8 (over x_hi, z), col: 16 (over y, x_lo, core).
Axes of the slice: x: 4 (x_hi: 2, x_lo: 2; x = x_hi * 2 + x_lo), y: 4, z: 4, core: 2. Of those that a mesh axis runs over, the one named last changes fastest.
Arguments:
- seq: bfloat16 [3072, 1024], P(('row', 'col')), may hold values from -6 to 6
- gain: float32 [1024], replicated, may hold values from 0.5 to 1.5
- beta: float32 [1024], replicated, may hold values from -3 to 3
- w_proj: bfloat16 [1024, 128], replicated, may hold values from -0.1875 to 0.1875
- b_proj: float32 [128], replicated, may hold values from -3 to 3
- w_out: bfloat16 [128, 128], replicated, may hold values from -0.5 to 0.5
- pair_grad: bfloat16 [3072, 3072, 128], P('row', 'col'), may hold values from -0.059814453 to 0.059814453
Outputs:
- d_seq: bfloat16 [3072, 1024], P(('row', 'col'))
- d_w_proj: float32 [1024, 128], replicated
- d_b_proj: float32 [128], replicated
- d_w_out: float32 [128, 128], replicated
- d_b_out: float32 [128], replicated
All inputs are finite; a program needn't handle non-finite values.
Results may differ from a plain program's by a relative error of at most 0.0065.
Values may be sent and summed in bfloat16 or wider, within the bound.
No kernel may reach another device: no remote copies, remote signals or barrier semaphores. Data moves between devices by JAX's collectives and lax.ppermute only.
A program may use at most 128 MiB of HBM per device.

v0:
```python
import jax
import jax.numpy as jnp
from jax import lax
from jax.sharding import PartitionSpec as P


def local(seq, gain, beta, w_proj, b_proj, w_out, pair_grad):
    inner = w_proj.shape[1] // 2
    row_idx = lax.axis_index("row")
    col_idx = lax.axis_index("col")
    rtile = pair_grad.shape[0]
    ctile = pair_grad.shape[1]
    source = seq.astype(jnp.float32)
    mean_val = jnp.mean(source, axis=1, keepdims=True)
    centred = source - mean_val
    variance = jnp.mean(centred * centred, axis=1, keepdims=True)
    inverse = 1.0 / jnp.sqrt(variance + 1e-05)
    normed = centred * inverse
    y_rows = (normed * gain + beta).astype(jnp.bfloat16)
    qk_rows = (jnp.dot(y_rows, w_proj, preferred_element_type=jnp.float32) + b_proj).astype(
        jnp.bfloat16
    )
    qk_all = lax.all_gather(qk_rows, ("row", "col"), axis=0, tiled=True)
    query = lax.dynamic_slice_in_dim(qk_all, row_idx * rtile, rtile, 0)[:, :inner].astype(
        jnp.float32
    )
    key_rows = lax.dynamic_slice_in_dim(qk_all, col_idx * ctile, ctile, 0)[:, inner:].astype(
        jnp.float32
    )
    key_ext = jnp.concatenate([key_rows, jnp.ones((ctile, inner), jnp.float32)], axis=1)
    key_twice = jnp.concatenate([key_rows, key_rows], axis=1)
    query_ext = jnp.concatenate([query, -jnp.ones((rtile, inner), jnp.float32)], axis=1)
    query_twice = jnp.concatenate([query, query], axis=1)
    big_g = lax.dot_general(
        pair_grad, w_out, (((2,), (1,)), ((), ())), preferred_element_type=jnp.float32
    )
    part_q = jnp.einsum("ijc,jc->ic", big_g, key_ext)
    part_k = jnp.einsum("ijc,ic->jc", big_g, query_ext)
    dq_tile = part_q[:, :inner] + part_q[:, inner:]
    dk_tile = part_k[:, :inner] + part_k[:, inner:]
    lanes = jnp.arange(2 * inner) < inner
    feats = jnp.where(
        lanes,
        query_twice[:, None, :] * key_twice[None, :, :],
        query_twice[:, None, :] - key_twice[None, :, :],
    ).astype(jnp.bfloat16)
    wout_term = lax.dot_general(
        feats, pair_grad, (((0, 1), (0, 1)), ((), ())), preferred_element_type=jnp.float32
    )
    bout_term = jnp.sum(pair_grad.astype(jnp.float32), axis=(0, 1))
    total_rows = qk_all.shape[0]
    blank = jnp.zeros((total_rows, 2 * inner), jnp.float32)
    dq_wide = jnp.concatenate([dq_tile, jnp.zeros((rtile, inner), jnp.float32)], axis=1)
    dk_wide = jnp.concatenate([jnp.zeros((ctile, inner), jnp.float32), dk_tile], axis=1)
    placed = lax.dynamic_update_slice(
        blank, dq_wide, (row_idx * rtile, 0)
    ) + lax.dynamic_update_slice(blank, dk_wide, (col_idx * ctile, 0))
    dqk = lax.psum_scatter(placed, ("row", "col"), scatter_dimension=0, tiled=True)
    bproj_term = jnp.sum(dqk, axis=0)
    dqk_b = dqk.astype(jnp.bfloat16)
    wproj_term = jnp.dot(y_rows.T, dqk_b, preferred_element_type=jnp.float32)
    d_w_proj, d_b_proj, d_w_out, d_b_out = lax.psum(
        (wproj_term, bproj_term, wout_term, bout_term), ("row", "col")
    )
    d_normed = jnp.dot(dqk_b, w_proj.T, preferred_element_type=jnp.float32) * gain
    d_seq = inverse * (
        d_normed
        - jnp.mean(d_normed, axis=1, keepdims=True)
        - normed * jnp.mean(d_normed * normed, axis=1, keepdims=True)
    )
    return (d_seq.astype(jnp.bfloat16), d_w_proj, d_b_proj, d_w_out, d_b_out)


def solution(mesh):
    in_specs = (P(("row", "col"), None), P(), P(), P(), P(), P(), P("row", "col", None))
    out_specs = (P(("row", "col"), None), P(), P(), P(), P())
    return jax.shard_map(local, mesh=mesh, in_specs=in_specs, out_specs=out_specs, check_vma=False)
```

profile of v0, /device:TPU:1, one launch (start us, length us, event | category | flops | bytes accessed | tf_op | source)
XLA Modules:
  0.0 1035.5 jit_solution(6509603591743042570)
XLA Ops:
  7.2 0.9 convert_reduce_fusion.1
  8.2 1.0 fusion.22
  9.2 1.0 fusion.10
  10.2 182.3 %all_gather.3 = bf16[3072,128]{1,0:T(8,128)(2,1)S(1)} all-gather(bf16[24,128]{1,0:T(8,128)(2,1)S(1)} %fusion.10), channel_id=1, replica_groups=mesh['row'=8,'col'=16] {'row','col'}, dimensions={0}, use_global_device_ids=true | all-gather | bytes 792576 | tf_op jit(solution)/shard_map/all_gather | solution.py:23
  192.7 0.1 pad_maximum_fusion
  192.8 36.1 %multiply_reduce_fusion.1 = (f32[128,384]{0,1:T(8,128)S(1)}, f32[384,192,128]{2,0,1:T(8,128)}) fusion(f32[128,192]{0,1:T(8,128)S(1)} %get-tuple-element.14, bf16[128,128]{1,0:T(8,128)(2,1)} %param.12, bf16[384,192,128]{2,1,0:T(8,128)(2,1)} %param.13), kind=kOutput, calls=%fused_computation.1 | convolution fusion | flops 2434744320 | bytes 56950784 | tf_op jit(solution)/shard_map/dot_general | solution.py:34
  229.0 15.7 %multiply_reduce_fusion = f32[128,192]{0,1:T(8,128)S(1)} fusion(f32[384,192,128]{2,0,1:T(8,128)} %get-tuple-element.16, f32[128,384]{0,1:T(8,128)S(1)} %get-tuple-element.12), kind=kLoop, calls=%fused_computation | loop fusion | flops 18849792 | bytes 38043648 | tf_op jit(solution)/shard_map/ijc,ic->jc/dot_general | solution.py:38
  244.8 0.1 slice_add_fusion
  244.9 0.1 broadcast_in_dim.5
  245.1 0.1 add_dynamic-update-slice_fusion
  245.2 1.2 copy-done.1
  246.4 0.1 copy.16
  246.6 9.7 select_convert_fusion.6
  256.3 11.7 %convert_reduce_fusion = f32[128]{0:T(128)S(1)} fusion(bf16[384,192,128]{2,1,0:T(8,128)(2,1)} %param.13), kind=kLoop, calls=%fused_computation.2 | loop fusion | flops 18874240 | bytes 18874880 | tf_op jit(solution)/shard_map/reduce_sum | solution.py:50
  268.0 40.3 %fusion.7 = f32[128,128]{1,0:T(8,128)} fusion(bf16[384,192,128]{2,1,0:T(8,128)(2,1)} %param.13, bf16[384,192,128]{0,2,1:T(8,128)(2,1)} %select_convert_fusion.6), kind=kOutput, calls=%fused_computation.12 | convolution fusion | flops 2415919104 | bytes 37814272 | tf_op jit(solution)/shard_map/dot_general | solution.py:47
  308.3 564.1 %reduce-scatter.5.cloned.1.call-done = f32[24,128]{1,0:T(8,128)} async-done(((f32[3072,128]{1,0:T(8,128)}), f32[24,128]{1,0:T(8,128)}) %reduce-scatter.5.cloned.1.call-update) | async-done | bytes 12304
  872.4 1.8 fusion.24
  874.3 1.1 fusion.29
  875.4 0.7 reduce_sum.58
  876.1 69.1 %all-reduce.5 = (f32[128]{0:T(128)}, f32[128]{0:T(128)}) all-reduce(f32[128]{0:T(128)S(1)} %reduce_sum.58, f32[128]{0:T(128)S(1)} %convert_reduce_fusion), channel_id=1, replica_groups=mesh['row'=8,'col'=16] {'row','col'}, use_global_device_ids=true, to_apply=%region_7.8 | all-reduce | flops 256 | bytes 2048 | tf_op jit(solution)/shard_map/psum | solution.py:62
  945.2 0.7 fusion.21
  946.0 78.9 %all-reduce.9.cloned.1.call-done = (f32[1024,128]{1,0:T(8,128)}, f32[128,128]{1,0:T(8,128)}) async-done(((f32[1024,128]{1,0:T(8,128)}, f32[128,128]{1,0:T(8,128)}), (f32[1024,128]{1,0:T(8,128)}, f32[128,128]{1,0:T(8,128)})) %all-reduce.9.cloned.1.call-update) | async-done | bytes 589840 | tf_op jit(solution)/shard_map/psum | solution.py:62
  1024.9 1.9 copy.45
  1026.8 1.5 copy.46
  (22 shorter events, 0.5 us)
Async XLA Ops:
  7.2 2.0 copy-start
  7.2 865.3 %reduce-scatter.5.cloned.1.call-start = ((), (), s32[]{:S(2)}) async-start(), calls=%async_computation.1 | async-start | bytes 1585152
  245.2 1.2 copy-start.1
  246.4 778.5 %all-reduce.9.cloned.1.call-start = ((), (), s32[]{:S(2)}) async-start(), calls=%async_computation.2 | async-start | bytes 1179648 | tf_op jit(solution)/shard_map/psum | solution.py:62
  267.9 604.5 %copy-start.2 = (bf16[24,1024]{1,0:T(8,128)(2,1)S(1)}, bf16[24,1024]{1,0:T(8,128)(2,1)}, u32[]{:S(2)}) copy-start(bf16[24,1024]{1,0:T(8,128)(2,1)} %param.7) | copy-start | bytes 147460
  267.9 604.5 %copy-start.3 = (f32[1024]{0:T(1024)S(1)}, f32[1024]{0:T(1024)}, u32[]{:S(2)}) copy-start(f32[1024]{0:T(1024)} %param.8) | copy-start | bytes 12292
  267.9 604.5 %copy-start.4 = (f32[1024]{0:T(1024)S(1)}, f32[1024]{0:T(1024)}, u32[]{:S(2)}) copy-start(f32[1024]{0:T(1024)} %param.9) | copy-start | bytes 12292
Sparse Core Ops, SparseCore 0:
  246.5 625.9 reduce-scatter.4
  878.6 146.2 all-reduce.8
where the time goes:
time: 1050 us; the launch traced here: 1040 us
  waiting for transfers between devices  643 us (61%)
  blocking collectives  251 us (24%)
  matrix products  80.4 us (8%)
  other arithmetic  41.1 us (4%)
  between operations  14.6 us (1%)
    unnamed x3, waiting for transfers between devices  564 us
    all_gather x1, blocking collectives, local(): qk_all = lax.all_gather(qk_rows, ('row', 'col'), axis=0, tiled=True)  182 us
    psum x1, waiting for transfers between devices, local(): lax.psum((wproj_term, bproj_term, wout_term, bout_term), ('row', 'col'))  78.9 us
    psum x1, blocking collectives, local(): lax.psum((wproj_term, bproj_term, wout_term, bout_term), ('row', 'col'))  69.1 us
    dot_general x1, matrix products, local(): lax.dot_general(feats, pair_grad, (((0, 1), (0, 1)), ((), ())), preferred...  40.3 us
    dot_general x1, matrix products, local(): lax.dot_general(pair_grad, w_out, (((2,), (1,)), ((), ())), preferred_ele...  36.1 us
  transfers between devices with their start and end apart: 2, of which 2 were waited for; matrix products, arithmetic and copies ran while one was open for 6% of the time, Pallas kernels for 0%

commit v1 on v0

v1 whole, which is shorter than its diff:
```python
import functools

import jax
import jax.numpy as jnp
from jax import lax
from jax.experimental import pallas as pl
from jax.experimental.pallas import tpu as pltpu
from jax.sharding import PartitionSpec as P

F32 = jnp.float32
BF16 = jnp.bfloat16
BOTH = ("row", "col")
CHUNK = 32


def _params(mib):
    return pltpu.CompilerParams(vmem_limit_bytes=mib * 2**20)


def _vmem(n):
    return [pl.BlockSpec(memory_space=pltpu.VMEM)] * n


def _norm(seq):
    source = seq.astype(F32)
    centred = source - jnp.mean(source, axis=1, keepdims=True)
    variance = jnp.mean(centred * centred, axis=1, keepdims=True)
    inverse = 1.0 / jnp.sqrt(variance + 1e-05)
    return centred * inverse, inverse


def _project_kernel(seq_ref, gain_ref, beta_ref, w_ref, b_ref, out_ref):
    normed, _ = _norm(seq_ref[...])
    y = (normed * gain_ref[...] + beta_ref[...]).astype(BF16)
    qk = (jnp.dot(y, w_ref[...], preferred_element_type=F32) + b_ref[...]).astype(BF16)
    out_ref[...] = jnp.broadcast_to(qk[None], out_ref.shape)


def _pair_kernel(
    qk_ref, w_ref, pg_hbm, dq_ref, dk_ref, dw_ref, db_ref,
    pg, sems, q2_s, qt_s, kt_s, k2_s, wbd_s, dq_s, r_s, dk_s, dwp_s, s_s,
):
    rows, cols, pair = pg.shape
    inner = pair // 2
    half = cols // 2
    n_chunks = rows // CHUNK

    def copy(ch):
        part = pl.ds(ch * CHUNK, CHUNK)
        return pltpu.make_async_copy(pg_hbm.at[part], pg.at[part], sems.at[ch])

    for ch in range(n_chunks):
        copy(ch).start()

    nq, shard = dq_ref.shape[0], dq_ref.shape[1]
    nk = dk_ref.shape[0]
    me_r = lax.axis_index("row")
    me_c = lax.axis_index("col")
    q = qk_ref[pl.ds(me_r * nq, nq)].astype(F32).reshape(rows, pair)[:, :inner]
    k = qk_ref[pl.ds(me_c * nk, nk)].astype(F32).reshape(cols, pair)[:, inner:]
    q2_s[...] = jnp.concatenate([q, q], axis=1)
    k2_s[...] = jnp.concatenate([k[:half], k[half:]], axis=1)
    qt = q.T
    for ch in range(n_chunks):
        qt_s[ch] = qt[:, ch * CHUNK : (ch + 1) * CHUNK]
    kt_s[...] = jnp.concatenate([k.T, jnp.ones((16, cols), F32)], axis=0).astype(BF16)
    wt = w_ref[...].astype(F32).T
    blank = jnp.zeros((pair, inner), F32)
    top = jnp.concatenate([wt[:, :inner], blank, wt[:, inner:], blank], axis=1)
    bottom = jnp.concatenate([blank, wt[:, :inner], blank, wt[:, inner:]], axis=1)
    wbd_s[...] = jnp.concatenate([top, bottom], axis=0).astype(BF16)
    dk_s[...] = jnp.zeros_like(dk_s)
    dwp_s[...] = jnp.zeros_like(dwp_s)
    s_s[...] = jnp.zeros_like(s_s)

    def chunk(ch, carry):
        copy(ch).wait()
        base = ch * CHUNK
        dk = dk_s[...]
        k2 = k2_s[...]
        for i in range(CHUNK):
            block = pg[base + i]
            g = jnp.dot(
                jnp.concatenate([block[:half], block[half:]], axis=1),
                wbd_s[...],
                preferred_element_type=F32,
            )
            gp, gd = g[:, :pair], g[:, pair:]
            dq_s[pl.ds(base + i, 1), :] = jnp.sum(gp * k2 + gd, axis=0, keepdims=True)
            dk = dk + (gp * q2_s[pl.ds(base + i, 1), :] - gd)
        dk_s[...] = dk
        dwp = dwp_s[...]
        s = s_s[...]
        for i in range(0, CHUNK, 2):
            a = jnp.dot(
                kt_s[...],
                jnp.concatenate([pg[base + i], pg[base + i + 1]], axis=1),
                preferred_element_type=F32,
            )
            a0, a1 = a[:inner, :pair], a[:inner, pair:]
            dwp = dwp + (a0 * qt_s[ch, :, i : i + 1] + a1 * qt_s[ch, :, i + 1 : i + 2])
            s = s + (a0 + a1)
            r_s[pl.ds(base + i, 1), :] = a[inner : inner + 1, :pair]
            r_s[pl.ds(base + i + 1, 1), :] = a[inner : inner + 1, pair:]
        dwp_s[...] = dwp
        s_s[...] = s
        return carry

    lax.fori_loop(0, n_chunks, chunk, 0)

    dq = dq_s[...]
    dq = dq[:, :inner] + dq[:, inner:]
    dq_ref[...] = jnp.concatenate([dq, jnp.zeros_like(dq)], axis=1).reshape(dq_ref.shape)
    dk = dk_s[...]
    dk = jnp.concatenate([dk[:, :inner], dk[:, inner:]], axis=0)
    dk_ref[...] = jnp.concatenate([dk, jnp.zeros_like(dk)], axis=1).reshape(dk_ref.shape)
    r = r_s[...]
    dw_ref[:inner, :] = dwp_s[...]
    dw_ref[inner:, :] = (
        lax.dot_general(
            q2_s[...][:, :inner], r, (((0,), (0,)), ((), ())),
            precision=lax.Precision.HIGHEST, preferred_element_type=F32,
        )
        - s_s[...]
    )
    db_ref[...] = jnp.sum(r, axis=0, keepdims=True)


def _split(x):
    high = x.astype(BF16).astype(F32)
    return high, x - high


def _grad_kernel(
    seq_ref, seqk_ref, gain_ref, beta_ref, dq_ref, dk_ref, dw_ref, db_ref,
    out_ref, dqb_ref, dkb_ref,
):
    inner = dqb_ref.shape[1]
    dq = jnp.sum(dq_ref[...], axis=0)[:, :inner]
    dk = jnp.sum(dk_ref[...], axis=0)[:, :inner]
    dq_b, dk_b = dq.astype(BF16), dk.astype(BF16)
    dqb_ref[...] = dq_b
    dkb_ref[...] = dk_b
    b_proj = jnp.concatenate(
        [jnp.sum(dq, axis=0, keepdims=True), jnp.sum(dk, axis=0, keepdims=True)], axis=1
    )
    y_q = (_norm(seq_ref[...])[0] * gain_ref[...] + beta_ref[...]).astype(BF16)
    y_k = (_norm(seqk_ref[...])[0] * gain_ref[...] + beta_ref[...]).astype(BF16)
    dims = (((0,), (0,)), ((), ()))
    w_proj = jnp.concatenate(
        [
            lax.dot_general(y_q, dq_b, dims, preferred_element_type=F32),
            lax.dot_general(y_k, dk_b, dims, preferred_element_type=F32),
        ],
        axis=1,
    )
    n = out_ref.shape[0]
    pair = out_ref.shape[2]
    w_hi, w_lo = _split(dw_ref[...])
    bo_hi, bo_lo = _split(db_ref[...])
    bp_hi, bp_lo = _split(b_proj)
    place = lax.broadcasted_iota(jnp.int32, (n, 8, pair), 1)
    lower = jnp.zeros((n, 8, pair), F32)
    for at, value in enumerate(
        (w_hi[:, None, :], w_lo[:, None, :], bo_hi[None], bo_lo[None], bp_hi[None], bp_lo[None])
    ):
        lower = jnp.where(place == at, jnp.broadcast_to(value, lower.shape), lower)
    out_ref[...] = jnp.concatenate([w_proj.reshape(n, 8, pair), lower], axis=1).astype(BF16)


def _reduce_kernel(x_ref, out_ref, bo_ref, bp_ref):
    total = jnp.sum(x_ref[...].astype(F32), axis=0)
    bo_ref[...] = total[10:11] + total[11:12]
    bp_ref[...] = total[12:13] + total[13:14]
    w_hi, w_lo = _split(total[8:9] + total[9:10])
    tile = jnp.concatenate([total[:8], w_hi, w_lo, jnp.zeros((6, total.shape[1]), F32)], axis=0)
    out_ref[...] = jnp.broadcast_to(tile.astype(BF16)[None], out_ref.shape)


def _unpack_kernel(x_ref, w_proj_ref, w_out_ref):
    x = x_ref[...].astype(F32)
    w_proj_ref[...] = x[:, :8].reshape(w_proj_ref.shape)
    w_out_ref[...] = x[:, 8] + x[:, 9]


def _seq_kernel(seq_ref, gain_ref, w_ref, dq_ref, dk_ref, out_ref):
    normed, inverse = _norm(seq_ref[...])
    dqk = jnp.concatenate([dq_ref[...], dk_ref[...]], axis=1)
    dn = (
        lax.dot_general(dqk, w_ref[...], (((1,), (1,)), ((), ())), preferred_element_type=F32)
        * gain_ref[...]
    )
    out_ref[...] = (
        inverse
        * (
            dn
            - jnp.mean(dn, axis=1, keepdims=True)
            - normed * jnp.mean(dn * normed, axis=1, keepdims=True)
        )
    ).astype(BF16)


def local(n_row, n_col, seq, gain, beta, w_proj, b_proj, w_out, pair_grad):
    shard, width = seq.shape
    pair = w_out.shape[1]
    inner = pair // 2
    rows, cols = pair_grad.shape[:2]
    n = n_row * n_col
    nq, nk = rows // shard, cols // shard
    gain = gain.reshape(1, width)
    beta = beta.reshape(1, width)
    shape = jax.ShapeDtypeStruct

    to_sum = []
    for owner in range(n):
        to_sum.append((owner, (owner % nk) * n_col + owner // nk))
    to_owner = [(b, a) for a, b in to_sum]

    seq_k = lax.ppermute(seq, BOTH, to_sum)
    qk = pl.pallas_call(
        _project_kernel,
        out_shape=shape((n, shard, pair), BF16),
        in_specs=_vmem(5),
        out_specs=pl.BlockSpec(memory_space=pltpu.VMEM),
        compiler_params=_params(32),
    )(seq, gain, beta, w_proj, b_proj.reshape(1, pair))
    qk_all = lax.all_to_all(qk, BOTH, 0, 0, tiled=True)

    dq_part, dk_part, dw_part, db_part = pl.pallas_call(
        _pair_kernel,
        out_shape=(
            shape((nq, shard, pair), F32),
            shape((nk, shard, pair), F32),
            shape((pair, pair), F32),
            shape((1, pair), F32),
        ),
        in_specs=_vmem(2) + [pl.BlockSpec(memory_space=pl.ANY)],
        out_specs=tuple(_vmem(4)),
        scratch_shapes=[
            pltpu.VMEM(pair_grad.shape, BF16),
            pltpu.SemaphoreType.DMA((rows // CHUNK,)),
            pltpu.VMEM((rows, pair), F32),
            pltpu.VMEM((rows // CHUNK, inner, CHUNK), F32),
            pltpu.VMEM((inner + 16, cols), BF16),
            pltpu.VMEM((cols // 2, pair), F32),
            pltpu.VMEM((2 * pair, 2 * pair), BF16),
            pltpu.VMEM((rows, pair), F32),
            pltpu.VMEM((rows, pair), F32),
            pltpu.VMEM((cols // 2, pair), F32),
            pltpu.VMEM((inner, pair), F32),
            pltpu.VMEM((inner, pair), F32),
        ],
        compiler_params=_params(40),
    )(qk_all, w_out, pair_grad)

    dq_in = lax.all_to_all(dq_part, "col", 0, 0, tiled=True)
    dk_in = lax.all_to_all(dk_part, "row", 0, 0, tiled=True)

    slots, dq_b, dk_b = pl.pallas_call(
        _grad_kernel,
        out_shape=(
            shape((n, 16, pair), BF16),
            shape((shard, inner), BF16),
            shape((shard, inner), BF16),
        ),
        in_specs=_vmem(8),
        out_specs=tuple(_vmem(3)),
        compiler_params=_params(40),
    )(seq, seq_k, gain, beta, dq_in, dk_in, dw_part, db_part)
    dk_own = lax.ppermute(dk_b, BOTH, to_owner)
    gathered = lax.all_to_all(slots, BOTH, 0, 0, tiled=True)

    reduced, d_b_out, d_b_proj = pl.pallas_call(
        _reduce_kernel,
        out_shape=(shape((n, 16, pair), BF16), shape((1, pair), F32), shape((1, pair), F32)),
        in_specs=_vmem(1),
        out_specs=tuple(_vmem(3)),
        compiler_params=_params(32),
    )(gathered)
    spread = lax.all_to_all(reduced, BOTH, 0, 0, tiled=True)

    d_seq = pl.pallas_call(
        _seq_kernel,
        out_shape=shape(seq.shape, BF16),
        in_specs=_vmem(5),
        out_specs=pl.BlockSpec(memory_space=pltpu.VMEM),
        compiler_params=_params(32),
    )(seq, gain, w_proj, dq_b, dk_own)

    d_w_proj, d_w_out = pl.pallas_call(
        _unpack_kernel,
        out_shape=(shape((width, pair), F32), shape((pair, pair), F32)),
        in_specs=_vmem(1),
        out_specs=tuple(_vmem(2)),
        compiler_params=_params(32),
    )(spread)
    return d_seq, d_w_proj, d_b_proj.reshape(pair), d_w_out, d_b_out.reshape(pair)


def solution(mesh):
    in_specs = (P(BOTH, None), P(), P(), P(), P(), P(), P("row", "col", None))
    out_specs = (P(BOTH, None), P(), P(), P(), P())
    body = functools.partial(local, mesh.shape["row"], mesh.shape["col"])
    return jax.shard_map(body, mesh=mesh, in_specs=in_specs, out_specs=out_specs, check_vma=False)
```

time: 1050 us -> 116 us (0.11); the launches traced: 1040 us -> 115 us
  waiting for transfers between devices: 643 us -> 13.6 us
  blocking collectives: 251 us -> 59.7 us
  matrix products: 80.4 us -> 0 us
  other arithmetic: 41.1 us -> 0 us
  Pallas kernels: 0 us -> 19.1 us
  starting transfers between devices: 0.08 us -> 17.6 us
  between operations: 14.6 us -> 0.72 us
    unnamed x3 -> x0, waiting for transfers between devices: 564 us -> none
    all_gather x1 -> x0, blocking collectives: 182 us -> none  [local(): qk_all = lax.all_gather(qk_rows, ('row', 'col'), axis=0, tiled=True)]
    dot_general x5 -> x0, matrix products: 80.4 us -> none  [the longest x1 40.3 us: local(): lax.dot_general(feats, pair_grad, (((0, 1), (0, 1)), ((), ())), preferred...]
    psum x1 -> x0, waiting for transfers between devices: 78.9 us -> none  [local(): lax.psum((wproj_term, bproj_term, wout_term, bout_term), ('row', 'col'))]
    psum x1 -> x0, blocking collectives: 69.1 us -> none  [local(): lax.psum((wproj_term, bproj_term, wout_term, bout_term), ('row', 'col'))]
    all_to_all x0 -> x3, blocking collectives: none -> 59.7 us  [the longest x1 27.5 us: local(): qk_all = lax.all_to_all(qk, BOTH, 0, 0, tiled=True)]
    dot_general x2 -> x0, other arithmetic: 25.5 us -> none  [the longest x1 15.7 us: local(): part_k = jnp.einsum('ijc,ic->jc', big_g, query_ext)]
    pallas_call x0 -> x6, Pallas kernels: none -> 19.1 us  [the longest x1 15.2 us: local(): pl.pallas_call(_pair_kernel, out_shape=(shape((nq, shard, pair), F32), sh...]
  transfers between devices with their start and end apart: 2 -> 4, of which waited for: 2 -> 3; matrix products, arithmetic and copies ran while one was open for 6% -> 0% of each run, Pallas kernels for 0% -> 1%
where the time goes in v1:
time: 116 us; the launch traced here: 115 us
  blocking collectives  59.7 us (51%)
  Pallas kernels  19.1 us (16%)
  starting transfers between devices  17.6 us (15%)
  waiting for transfers between devices  13.6 us (12%)
  local copies, waits for them, and re-layouts  4.55 us (4%)
    all_to_all x1, blocking collectives, local(): qk_all = lax.all_to_all(qk, BOTH, 0, 0, tiled=True)  27.5 us
    all_to_all x1, blocking collectives, local(): gathered = lax.all_to_all(slots, BOTH, 0, 0, tiled=True)  22.6 us
    pallas_call x1, Pallas kernels, local(): pl.pallas_call(_pair_kernel, out_shape=(shape((nq, shard, pair), F32), sh...  15.2 us
    all_to_all x1, blocking collectives, local(): dk_in = lax.all_to_all(dk_part, 'row', 0, 0, tiled=True)  9.53 us
    all_to_all x1, waiting for transfers between devices, local(): spread = lax.all_to_all(reduced, BOTH, 0, 0, tiled=True)  6.65 us
    ppermute x1, waiting for transfers between devices, local(): seq_k = lax.ppermute(seq, BOTH, to_sum)  6.15 us
    all_to_all x1, starting transfers between devices, local(): dq_in = lax.all_to_all(dq_part, 'col', 0, 0, tiled=True)  5.36 us
    ppermute x1, starting transfers between devices, local(): dk_own = lax.ppermute(dk_b, BOTH, to_owner)  5.05 us
  transfers between devices with their start and end apart: 4, of which 3 were waited for; matrix products, arithmetic and copies ran while one was open for 0% of the time, Pallas kernels for 1%

profile of v1, /device:TPU:1, one launch (start us, length us, event | category | flops | bytes accessed | tf_op | source)
XLA Modules:
  0.0 115.2 jit_solution(14317699393357082955)
XLA Ops:
  0.7 0.9 copy-done
  1.6 0.8 copy-done.2
  2.4 0.7 copy-done.4
  3.1 0.7 copy-done.7
  3.8 0.7 copy-done.9
  4.4 0.4 shard_map.110
  4.8 27.5 %all_to_all.25.qk_ref = bf16[128,24,128]{2,1,0:T(8,128)(2,1)S(1)} all-to-all(bf16[128,24,128]{2,1,0:T(8,128)(2,1)S(1)} %shard_map.110), channel_id=1, replica_groups=mesh['row'=8,'col'=16] {'row','col'}, dimensions={0} | all-to-all | bytes 1572864 | tf_op jit(solution)/shard_map/all_to_all | solution.py:227
  32.4 0.8 copy-done.6
  33.1 15.2 %shard_map.111 = (f32[16,24,128]{2,1,0:T(8,128)}, f32[8,24,128]{2,1,0:T(8,128)S(1)}, f32[128,128]{1,0:T(8,128)S(1)}, f32[1,128]{1,0:T(1,128)S(1)}) custom-call(bf16[128,24,128]{2,1,0:T(8,128)(2,1)S(1)} %all_to_all.25.qk_ref, bf16[128,128]{1,0:T(8,128)(2,1)S(1)} %copy-done.6, bf16[384,192,128]{2,1,0:T(8,128)(2,1)} %pg_hbm.1), custom_call_target="tpu_custom_call" | custom-call | tf_op jit(solution)/shard_map/pallas_call | solution.py:229
  48.4 9.5 %all_to_all.26.dk_ref = f32[8,24,128]{2,1,0:T(8,128)S(1)} all-to-all(f32[8,24,128]{2,1,0:T(8,128)S(1)} %get-tuple-element.18), channel_id=1, replica_groups=mesh['row'=8,'col'=16] {'row'}, dimensions={0} | all-to-all | bytes 196608 | tf_op jit(solution)/shard_map/all_to_all | solution.py:257
  57.9 5.4 %all-to-all-start.1 = ((f32[16,24,128]{2,1,0:T(8,128)}), f32[16,24,128]{2,1,0:T(8,128)S(1)}, u32[]{:S(2)}, u32[]{:S(2)}) async-start(f32[16,24,128]{2,1,0:T(8,128)} %get-tuple-element.17), calls=%async_computation.1 | async-start | bytes 393216 | tf_op jit(solution)/shard_map/all_to_all | solution.py:256
  63.3 2.3 %collective-permute-start = (bf16[24,1024]{1,0:T(8,128)(2,1)S(1)}, bf16[24,1024]{1,0:T(8,128)(2,1)S(1)}, u32[]{:S(2)}, u32[]{:S(2)}) collective-permute-start(bf16[24,1024]{1,0:T(8,128)(2,1)S(1)} %copy-done.3), channel_id=1, source_target_pairs={{0,0},{1,16},{2,32},{3,48},{4,64},{5,80},{6,96},{7,112},{8,1},{9,1... | collective-permute-start | bytes 147464 | tf_op jit(solution)/shard_map/ppermute | solution.py:219
  65.6 6.1 %collective-permute-done.seqk_ref = bf16[24,1024]{1,0:T(8,128)(2,1)S(1)} collective-permute-done((bf16[24,1024]{1,0:T(8,128)(2,1)S(1)}, bf16[24,1024]{1,0:T(8,128)(2,1)S(1)}, u32[]{:S(2)}, u32[]{:S(2)}) %collective-permute-start) | collective-permute-done | bytes 49184 | tf_op jit(solution)/shard_map/ppermute | solution.py:219
  71.7 0.0 all-to-all-done.1.dq_ref
  71.7 0.0 copy-done.8
  71.8 0.6 shard_map.112
  72.4 22.6 %all_to_all.27.x_ref = bf16[128,16,128]{2,1,0:T(8,128)(2,1)S(1)} all-to-all(bf16[128,16,128]{2,1,0:T(8,128)(2,1)S(1)} %get-tuple-element.23), channel_id=1, replica_groups=mesh['row'=8,'col'=16] {'row','col'}, dimensions={0} | all-to-all | bytes 1048576 | tf_op jit(solution)/shard_map/all_to_all | solution.py:271
  95.0 1.0 shard_map.114
  96.0 4.9 %all-to-all-start.4 = ((bf16[128,16,128]{2,1,0:T(8,128)(2,1)}), bf16[128,16,128]{2,1,0:T(8,128)(2,1)S(1)}, u32[]{:S(2)}, u32[]{:S(2)}) async-start(bf16[128,16,128]{2,1,0:T(8,128)(2,1)} %get-tuple-element.24), calls=%async_computation.4 | async-start | bytes 1048576 | tf_op jit(solution)/shard_map/all_to_all | solution.py:280
  100.9 5.1 %collective-permute-start.1 = (bf16[24,64]{1,0:T(8,128)(2,1)S(1)}, bf16[24,64]{1,0:T(8,128)(2,1)S(1)}, u32[]{:S(2)}, u32[]{:S(2)}) collective-permute-start(bf16[24,64]{1,0:T(8,128)(2,1)S(1)} %get-tuple-element.22), channel_id=1, source_target_pairs={{0,0},{16,1},{32,2},{48,3},{64,4},{80,5},{96,6},{112,7},{1,8},{17,... | collective-permute-start | bytes 9224 | tf_op jit(solution)/shard_map/ppermute | solution.py:270
  105.9 0.8 collective-permute-done.1.dk_ref
  106.7 0.9 shard_map.113
  107.6 6.7 %all-to-all-done.4.x_ref = bf16[128,16,128]{2,1,0:T(8,128)(2,1)S(1)} async-done(((bf16[128,16,128]{2,1,0:T(8,128)(2,1)}), bf16[128,16,128]{2,1,0:T(8,128)(2,1)S(1)}, u32[]{:S(2)}, u32[]{:S(2)}) %all-to-all-start.4) | async-done | bytes 524320 | tf_op jit(solution)/shard_map/all_to_all | solution.py:280
  114.3 0.9 shard_map.115
  (13 shorter events, 0.0 us)
Async XLA Ops:
  0.6 71.1 %copy-start.5 = (f32[1024]{0:T(1024)S(1)}, f32[1024]{0:T(1024)}, u32[]{:S(2)}) copy-start(f32[1024]{0:T(1024)} %param.8) | copy-start | bytes 12292
  0.6 1.0 copy-start
  1.6 0.8 copy-start.2
  2.4 0.7 copy-start.4
  3.1 0.7 copy-start.7
  3.8 0.7 copy-start.9
  4.4 58.9 %copy-start.3 = (bf16[24,1024]{1,0:T(8,128)(2,1)S(1)}, bf16[24,1024]{1,0:T(8,128)(2,1)}, u32[]{:S(2)}) copy-start(bf16[24,1024]{1,0:T(8,128)(2,1)} %seq_ref.5) | copy-start | bytes 147460
  4.4 67.3 %copy-start.8 = (f32[1024]{0:T(1024)S(1)}, f32[1024]{0:T(1024)}, u32[]{:S(2)}) copy-start(f32[1024]{0:T(1024)} %param.9) | copy-start | bytes 12292
  4.4 102.3 %copy-start.1 = (bf16[1024,128]{1,0:T(8,128)(2,1)S(1)}, bf16[1024,128]{1,0:T(8,128)(2,1)}, u32[]{:S(2)}) copy-start(bf16[1024,128]{1,0:T(8,128)(2,1)} %w_ref.5) | copy-start | bytes 786436
  32.4 0.8 copy-start.6
  57.9 13.8 %all-to-all-start.1 = ((f32[16,24,128]{2,1,0:T(8,128)}), f32[16,24,128]{2,1,0:T(8,128)S(1)}, u32[]{:S(2)}, u32[]{:S(2)}) async-start(f32[16,24,128]{2,1,0:T(8,128)} %get-tuple-element.17), calls=%async_computation.1 | async-start | bytes 393216 | tf_op jit(solution)/shard_map/all_to_all | solution.py:256
  63.3 8.5 %collective-permute-start = (bf16[24,1024]{1,0:T(8,128)(2,1)S(1)}, bf16[24,1024]{1,0:T(8,128)(2,1)S(1)}, u32[]{:S(2)}, u32[]{:S(2)}) collective-permute-start(bf16[24,1024]{1,0:T(8,128)(2,1)S(1)} %copy-done.3), channel_id=1, source_target_pairs={{0,0},{1,16},{2,32},{3,48},{4,64},{5,80},{6,96},{7,112},{8,1},{9,1... | collective-permute-start | bytes 147464 | tf_op jit(solution)/shard_map/ppermute | solution.py:219
  96.0 18.3 %all-to-all-start.4 = ((bf16[128,16,128]{2,1,0:T(8,128)(2,1)}), bf16[128,16,128]{2,1,0:T(8,128)(2,1)S(1)}, u32[]{:S(2)}, u32[]{:S(2)}) async-start(bf16[128,16,128]{2,1,0:T(8,128)(2,1)} %get-tuple-element.24), calls=%async_computation.4 | async-start | bytes 1048576 | tf_op jit(solution)/shard_map/all_to_all | solution.py:280
  100.9 5.8 %collective-permute-start.1 = (bf16[24,64]{1,0:T(8,128)(2,1)S(1)}, bf16[24,64]{1,0:T(8,128)(2,1)S(1)}, u32[]{:S(2)}, u32[]{:S(2)}) collective-permute-start(bf16[24,64]{1,0:T(8,128)(2,1)S(1)} %get-tuple-element.22), channel_id=1, source_target_pairs={{0,0},{16,1},{32,2},{48,3},{64,4},{80,5},{96,6},{112,7},{1,8},{17,... | collective-permute-start | bytes 9224 | tf_op jit(solution)/shard_map/ppermute | solution.py:270

commit v2 on v1

v2 whole, which is shorter than its diff:
```python
import functools

import jax
import jax.numpy as jnp
from jax import lax
from jax.experimental import pallas as pl
from jax.experimental.pallas import tpu as pltpu
from jax.sharding import PartitionSpec as P

F32 = jnp.float32
BF16 = jnp.bfloat16
BOTH = ("row", "col")
CHUNK = 48


def _params(mib):
    return pltpu.CompilerParams(vmem_limit_bytes=mib * 2**20)


def _norm(seq):
    source = seq.astype(F32)
    centred = source - jnp.mean(source, axis=1, keepdims=True)
    variance = jnp.mean(centred * centred, axis=1, keepdims=True)
    inverse = 1.0 / jnp.sqrt(variance + 1e-05)
    return centred * inverse, inverse


def _fetch(pairs, sems):
    copies = [pltpu.make_async_copy(a, b, sems.at[n]) for n, (a, b) in enumerate(pairs)]
    for c in copies:
        c.start()
    for c in copies:
        c.wait()


def _project_kernel(
    seq_hbm, gain_hbm, beta_hbm, w_hbm, b_hbm, out_ref, seq_s, gain_s, beta_s, w_s, b_s, sems
):
    _fetch(
        [(seq_hbm, seq_s), (gain_hbm, gain_s), (beta_hbm, beta_s), (w_hbm, w_s), (b_hbm, b_s)],
        sems,
    )
    normed, _ = _norm(seq_s[...])
    y = (normed * gain_s[...] + beta_s[...]).astype(BF16)
    qk = (jnp.dot(y, w_s[...], preferred_element_type=F32) + b_s[...]).astype(BF16)
    out_ref[...] = jnp.broadcast_to(qk[None], out_ref.shape)


def _tile_copies(pg_hbm, pg, sems):
    def copy(ch):
        part = pl.ds(ch * CHUNK, CHUNK)
        return pltpu.make_async_copy(pg_hbm.at[part], pg.at[part], sems.at[ch])

    for ch in range(pg.shape[0] // CHUNK):
        copy(ch).start()
    return copy


def _totals_kernel(pg_hbm, rc_ref, pg, sems):
    rows, cols, pair = pg.shape
    copy = _tile_copies(pg_hbm, pg, sems)
    over_i = pl.ds(rows, cols)
    rc_ref[over_i] = jnp.zeros((cols, pair), F32)

    def chunk(ch, carry):
        copy(ch).wait()
        base = ch * CHUNK
        total = rc_ref[over_i]
        for i in range(CHUNK):
            block = pg[base + i].astype(F32)
            rc_ref[pl.ds(base + i, 1), :] = jnp.sum(block, axis=0, keepdims=True)
            total = total + block
        rc_ref[over_i] = total
        return carry

    lax.fori_loop(0, rows // CHUNK, chunk, 0)


def _own_qk(qk_ref, nq, nk):
    shard, pair = qk_ref.shape[1:]
    inner = pair // 2
    me_r = lax.axis_index("row")
    me_c = lax.axis_index("col")
    q = qk_ref[pl.ds(me_r * nq, nq)].astype(F32).reshape(nq * shard, pair)[:, :inner]
    k = qk_ref[pl.ds(me_c * nk, nk)].astype(F32).reshape(nk * shard, pair)[:, inner:]
    return q, k


def _sums_kernel(
    nq, nk, qk_ref, rc_ref, w_hbm, pg_hbm, out_ref, bp_ref,
    pg, sems, w_s, w_sem, wbd_s, q2_s, k2_s, dq_s, dk_s,
):
    rows, cols, pair = pg.shape
    inner, half = pair // 2, cols // 2
    shard = out_ref.shape[1]
    copy = _tile_copies(pg_hbm, pg, sems)
    _fetch([(w_hbm, w_s)], w_sem)
    q, k = _own_qk(qk_ref, nq, nk)
    q2_s[...] = jnp.concatenate([q, q], axis=1)
    k2_s[...] = jnp.concatenate([k[:half], k[half:]], axis=1)
    wt = w_s[...].astype(F32).T
    blank = jnp.zeros((pair, inner), F32)
    top = jnp.concatenate([wt[:, :inner], blank], axis=1)
    bottom = jnp.concatenate([blank, wt[:, :inner]], axis=1)
    wbd_s[...] = jnp.concatenate([top, bottom], axis=0).astype(BF16)
    gd = jnp.dot(
        rc_ref[...], wt[:, inner:], precision=lax.Precision.HIGHEST, preferred_element_type=F32
    )
    dk_s[...] = jnp.zeros_like(dk_s)
    out_ref[...] = jnp.zeros_like(out_ref)

    def chunk(ch, carry):
        copy(ch).wait()
        base = ch * CHUNK
        dk = dk_s[...]
        k2 = k2_s[...]
        for i in range(CHUNK):
            block = pg[base + i]
            g = jnp.dot(
                jnp.concatenate([block[:half], block[half:]], axis=1),
                wbd_s[...],
                preferred_element_type=F32,
            )
            dq_s[pl.ds(base + i, 1), :] = jnp.sum(g * k2, axis=0, keepdims=True)
            dk = dk + g * q2_s[pl.ds(base + i, 1), :]
        dk_s[...] = dk
        return carry

    lax.fori_loop(0, rows // CHUNK, chunk, 0)
    dq = dq_s[...]
    dq = dq[:, :inner] + dq[:, inner:] + gd[:rows]
    dk = dk_s[...]
    dk = jnp.concatenate([dk[:, :inner], dk[:, inner:]], axis=0) - gd[rows:]
    bp_ref[...] = jnp.concatenate(
        [jnp.sum(dq, axis=0, keepdims=True), jnp.sum(dk, axis=0, keepdims=True)], axis=1
    )
    dq = jnp.concatenate([dq, jnp.zeros_like(dq)], axis=1).reshape(nq, shard, pair)
    dk = jnp.concatenate([jnp.zeros_like(dk), dk], axis=1).reshape(nk, shard, pair)
    at_q = pl.ds(lax.axis_index("row") * nq, nq)
    at_k = pl.ds(lax.axis_index("col") * nk, nk)
    out_ref[at_q] = dq.astype(BF16)
    out_ref[at_k] = (out_ref[at_k].astype(F32) + dk).astype(BF16)


def _weight_kernel(
    nq, nk, qk_ref, rc_ref, pg_hbm, dw_ref, db_ref, pg, sems, qt_s, kt_s, dwp_s
):
    rows, cols, pair = pg.shape
    inner = pair // 2
    n_chunks = rows // CHUNK
    copy = _tile_copies(pg_hbm, pg, sems)
    q, k = _own_qk(qk_ref, nq, nk)
    qt, kt = q.T, k.T
    for ch in range(n_chunks):
        qt_s[ch] = qt[:, ch * CHUNK : (ch + 1) * CHUNK]
    kt_s[...] = kt.astype(BF16)
    dwp_s[...] = jnp.zeros_like(dwp_s)
    rc = rc_ref[...]
    dw_ref[inner:, :] = jnp.dot(
        jnp.concatenate([qt, -kt], axis=1),
        rc,
        precision=lax.Precision.HIGHEST,
        preferred_element_type=F32,
    )
    db_ref[...] = jnp.sum(rc[:rows], axis=0, keepdims=True)

    def chunk(ch, carry):
        copy(ch).wait()
        base = ch * CHUNK
        dwp = dwp_s[...]
        for i in range(0, CHUNK, 2):
            a = jnp.dot(
                kt_s[...],
                jnp.concatenate([pg[base + i], pg[base + i + 1]], axis=1),
                preferred_element_type=F32,
            )
            dwp = dwp + (
                a[:, :pair] * qt_s[ch, :, i : i + 1] + a[:, pair:] * qt_s[ch, :, i + 1 : i + 2]
            )
        dwp_s[...] = dwp
        return carry

    lax.fori_loop(0, n_chunks, chunk, 0)
    dw_ref[:inner, :] = dwp_s[...]


def _split(x):
    high = x.astype(BF16).astype(F32)
    return high, x - high


def _grad_kernel(
    seq_ref, gain_ref, beta_ref, dqk_ref, dw_ref, db_ref, bp_ref, out_ref, dqkb_ref
):
    dqk_b = jnp.sum(dqk_ref[...].astype(F32), axis=0).astype(BF16)
    dqkb_ref[...] = dqk_b
    y = (_norm(seq_ref[...])[0] * gain_ref[...] + beta_ref[...]).astype(BF16)
    w_proj = lax.dot_general(y, dqk_b, (((0,), (0,)), ((), ())), preferred_element_type=F32)
    n = out_ref.shape[0]
    pair = out_ref.shape[2]
    w_hi, w_lo = _split(dw_ref[...])
    bo_hi, bo_lo = _split(db_ref[...])
    bp_hi, bp_lo = _split(bp_ref[...])
    place = lax.broadcasted_iota(jnp.int32, (n, 8, pair), 1)
    lower = jnp.zeros((n, 8, pair), F32)
    for at, value in enumerate(
        (w_hi[:, None, :], w_lo[:, None, :], bo_hi[None], bo_lo[None], bp_hi[None], bp_lo[None])
    ):
        lower = jnp.where(place == at, jnp.broadcast_to(value, lower.shape), lower)
    out_ref[...] = jnp.concatenate([w_proj.reshape(n, 8, pair), lower], axis=1).astype(BF16)


def _reduce_kernel(x_ref, out_ref, bo_ref, bp_ref):
    total = jnp.sum(x_ref[...].astype(F32), axis=0)
    bo_ref[...] = total[10:11] + total[11:12]
    bp_ref[...] = total[12:13] + total[13:14]
    w_hi, w_lo = _split(total[8:9] + total[9:10])
    tile = jnp.concatenate([total[:8], w_hi, w_lo, jnp.zeros((6, total.shape[1]), F32)], axis=0)
    out_ref[...] = jnp.broadcast_to(tile.astype(BF16)[None], out_ref.shape)


def _unpack_kernel(x_ref, w_proj_ref, w_out_ref):
    x = x_ref[...].astype(F32)
    w_proj_ref[...] = x[:, :8].reshape(w_proj_ref.shape)
    w_out_ref[...] = x[:, 8] + x[:, 9]


def _seq_kernel(seq_ref, gain_ref, w_ref, dqk_ref, out_ref):
    normed, inverse = _norm(seq_ref[...])
    dqk = dqk_ref[...]
    dn = (
        lax.dot_general(dqk, w_ref[...], (((1,), (1,)), ((), ())), preferred_element_type=F32)
        * gain_ref[...]
    )
    out_ref[...] = (
        inverse
        * (
            dn
            - jnp.mean(dn, axis=1, keepdims=True)
            - normed * jnp.mean(dn * normed, axis=1, keepdims=True)
        )
    ).astype(BF16)


def local(n_row, n_col, seq, gain, beta, w_proj, b_proj, w_out, pair_grad):
    shard, width = seq.shape
    pair = w_out.shape[1]
    inner = pair // 2
    rows, cols = pair_grad.shape[:2]
    n = n_row * n_col
    nq, nk = rows // shard, cols // shard
    gain = gain.reshape(1, width)
    beta = beta.reshape(1, width)
    shape = jax.ShapeDtypeStruct

    vmem = pl.BlockSpec(memory_space=pltpu.VMEM)
    hbm = pl.BlockSpec(memory_space=pltpu.HBM)
    tile = [pltpu.VMEM(pair_grad.shape, BF16), pltpu.SemaphoreType.DMA((rows // CHUNK,))]

    qk = pl.pallas_call(
        _project_kernel,
        out_shape=shape((n, shard, pair), BF16),
        in_specs=[hbm] * 5,
        out_specs=vmem,
        scratch_shapes=[
            pltpu.VMEM((shard, width), BF16),
            pltpu.VMEM((1, width), F32),
            pltpu.VMEM((1, width), F32),
            pltpu.VMEM((width, pair), BF16),
            pltpu.VMEM((1, pair), F32),
            pltpu.SemaphoreType.DMA((5,)),
        ],
        compiler_params=_params(60),
    )(seq, gain, beta, w_proj, b_proj.reshape(1, pair))
    qk_all = lax.all_to_all(qk, BOTH, 0, 0, tiled=True)

    rc = pl.pallas_call(
        _totals_kernel,
        out_shape=shape((rows + cols, pair), F32),
        in_specs=[hbm],
        out_specs=vmem,
        scratch_shapes=tile,
        compiler_params=_params(60),
        cost_estimate=pl.CostEstimate(
            flops=4 * rows * cols * pair * pair, bytes_accessed=3 * rows * cols * pair, transcendentals=0
        ),
    )(pair_grad)

    dqk_part, bp_part = pl.pallas_call(
        functools.partial(_sums_kernel, nq, nk),
        out_shape=(shape((n, shard, pair), BF16), shape((1, pair), F32)),
        in_specs=[vmem, vmem, hbm, hbm],
        out_specs=(vmem,) * 2,
        scratch_shapes=tile
        + [
            pltpu.VMEM((pair, pair), BF16),
            pltpu.SemaphoreType.DMA((1,)),
            pltpu.VMEM((2 * pair, pair), BF16),
            pltpu.VMEM((rows, pair), F32),
            pltpu.VMEM((cols // 2, pair), F32),
            pltpu.VMEM((rows, pair), F32),
            pltpu.VMEM((cols // 2, pair), F32),
        ],
        compiler_params=_params(40),
    )(qk_all, rc, w_out, pair_grad)
    dqk_in = lax.all_to_all(dqk_part, BOTH, 0, 0, tiled=True)

    dw_part, db_part = pl.pallas_call(
        functools.partial(_weight_kernel, nq, nk),
        out_shape=(shape((pair, pair), F32), shape((1, pair), F32)),
        in_specs=[vmem, vmem, hbm],
        out_specs=(vmem,) * 2,
        scratch_shapes=tile
        + [
            pltpu.VMEM((rows // CHUNK, inner, CHUNK), F32),
            pltpu.VMEM((inner, cols), BF16),
            pltpu.VMEM((inner, pair), F32),
        ],
        compiler_params=_params(40),
        cost_estimate=pl.CostEstimate(
            flops=4 * rows * cols * pair * pair, bytes_accessed=2 * rows * cols * pair, transcendentals=0
        ),
    )(qk_all, rc, pair_grad)

    slots, dqk_b = pl.pallas_call(
        _grad_kernel,
        out_shape=(shape((n, 16, pair), BF16), shape((shard, pair), BF16)),
        in_specs=[vmem] * 7,
        out_specs=(vmem,) * 2,
        compiler_params=_params(32),
    )(seq, gain, beta, dqk_in, dw_part, db_part, bp_part)
    gathered = lax.all_to_all(slots, BOTH, 0, 0, tiled=True)

    reduced, d_b_out, d_b_proj = pl.pallas_call(
        _reduce_kernel,
        out_shape=(shape((n, 16, pair), BF16), shape((1, pair), F32), shape((1, pair), F32)),
        in_specs=[vmem],
        out_specs=(vmem,) * 3,
        compiler_params=_params(32),
    )(gathered)
    spread = lax.all_to_all(reduced, BOTH, 0, 0, tiled=True)

    d_seq = pl.pallas_call(
        _seq_kernel,
        out_shape=shape(seq.shape, BF16),
        in_specs=[vmem] * 4,
        out_specs=vmem,
        compiler_params=_params(32),
    )(seq, gain, w_proj, dqk_b)

    d_w_proj, d_w_out = pl.pallas_call(
        _unpack_kernel,
        out_shape=(shape((width, pair), F32), shape((pair, pair), F32)),
        in_specs=[vmem],
        out_specs=(vmem,) * 2,
        compiler_params=_params(32),
    )(spread)
    return d_seq, d_w_proj, d_b_proj.reshape(pair), d_w_out, d_b_out.reshape(pair)


def solution(mesh):
    in_specs = (P(BOTH, None), P(), P(), P(), P(), P(), P("row", "col", None))
    out_specs = (P(BOTH, None), P(), P(), P(), P())
    body = functools.partial(local, mesh.shape["row"], mesh.shape["col"])
    return jax.shard_map(body, mesh=mesh, in_specs=in_specs, out_specs=out_specs, check_vma=False)
```

time: 116 us -> 101 us (0.87)
  blocking collectives: 59.7 us -> 18.1 us
  waiting for transfers between devices: 13.6 us -> 29.7 us
  Pallas kernels: 19.1 us -> 30.2 us
  starting transfers between devices: 17.6 us -> 21.3 us
  local copies, waits for them, and re-layouts: 4.55 us -> 0.99 us
    all_to_all x2 -> x0, blocking collectives: 37.1 us -> none  [the longest x1 27.5 us: local(): qk_all = lax.all_to_all(qk, BOTH, 0, 0, tiled=True)]
    all_to_all x1 -> x2, waiting for transfers between devices: 0.01 us -> 17.2 us  [the longest x1 8.81 us: local(): dqk_in = lax.all_to_all(dqk_part, BOTH, 0, 0, tiled=True)]
    all_to_all x1 -> x2, starting transfers between devices: 5.36 us -> 16.4 us  [the longest x1 11.5 us: local(): qk_all = lax.all_to_all(qk, BOTH, 0, 0, tiled=True)]
    pallas_call x2 -> x4, Pallas kernels: 16.2 us -> 25.5 us  [the longest x1 9.37 us: local(): pl.pallas_call(functools.partial(_sums_kernel, nq, nk), out_shape=(shape(...]
    ppermute x2 -> x0, starting transfers between devices: 7.35 us -> none  [the longest x1 5.05 us: local(): dk_own = lax.ppermute(dk_b, BOTH, to_owner)]
    ppermute x2 -> x0, waiting for transfers between devices: 6.92 us -> none  [the longest x1 6.15 us: local(): seq_k = lax.ppermute(seq, BOTH, to_sum)]
    all_to_all x1, waiting for transfers between devices: 6.65 us -> 12.5 us  [local(): spread = lax.all_to_all(reduced, BOTH, 0, 0, tiled=True)]
    all_to_all x1, blocking collectives: 22.6 us -> 18.1 us  [local(): gathered = lax.all_to_all(slots, BOTH, 0, 0, tiled=True)]
  transfers between devices with their start and end apart: 4 -> 3, of which waited for: 3 -> 3; matrix products, arithmetic and copies ran while one was open for 0% -> 0% of each run, Pallas kernels for 1% -> 16%
where the time goes in v2:
time: 101 us
  Pallas kernels  30.2 us (30%)
  waiting for transfers between devices  29.7 us (29%)
  starting transfers between devices  21.3 us (21%)
  blocking collectives  18.1 us (18%)
    all_to_all x1, blocking collectives, local(): gathered = lax.all_to_all(slots, BOTH, 0, 0, tiled=True)  18.1 us
    all_to_all x1, waiting for transfers between devices, local(): spread = lax.all_to_all(reduced, BOTH, 0, 0, tiled=True)  12.5 us
    all_to_all x1, starting transfers between devices, local(): qk_all = lax.all_to_all(qk, BOTH, 0, 0, tiled=True)  11.5 us
    pallas_call x1, Pallas kernels, local(): pl.pallas_call(functools.partial(_sums_kernel, nq, nk), out_shape=(shape(...  9.37 us
    all_to_all x1, waiting for transfers between devices, local(): dqk_in = lax.all_to_all(dqk_part, BOTH, 0, 0, tiled=True)  8.81 us
    all_to_all x1, waiting for transfers between devices, local(): qk_all = lax.all_to_all(qk, BOTH, 0, 0, tiled=True)  8.42 us
    pallas_call x1, Pallas kernels, local(): pl.pallas_call(_totals_kernel, out_shape=shape((rows + cols, pair), F32),...  7.81 us
    pallas_call x1, Pallas kernels, local(): pl.pallas_call(functools.partial(_weight_kernel, nq, nk), out_shape=(shap...  7.41 us
  transfers between devices with their start and end apart: 3, of which 3 were waited for; matrix products, arithmetic and copies ran while one was open for 0% of the time, Pallas kernels for 16%

profile of v2, /device:TPU:1, one launch (start us, length us, event | category | flops | bytes accessed | tf_op | source)
XLA Modules:
  0.0 101.1 jit_solution(5087499078423317173)
XLA Ops:
  0.6 0.0 copy-start.5
  0.6 2.3 %shard_map.110 = bf16[128,24,128]{2,1,0:T(8,128)(2,1)} custom-call(bf16[24,1024]{1,0:T(8,128)(2,1)} %seq_ref.3, f32[1,1024]{1,0:T(1,128)} %bitcast.5, f32[1,1024]{1,0:T(1,128)} %bitcast.8, bf16[1024,128]{1,0:T(8,128)(2,1)} %w_ref.1, f32[1,128]{1,0:T(1,128)} %bitcast.10), custom_call_target="tpu_custom_call" | custom-call | tf_op jit(solution)/shard_map/pallas_call | solution.py:260
  3.0 11.5 %all-to-all-start = ((bf16[128,24,128]{2,1,0:T(8,128)(2,1)}), bf16[128,24,128]{2,1,0:T(8,128)(2,1)S(1)}, u32[]{:S(2)}, u32[]{:S(2)}) async-start(bf16[128,24,128]{2,1,0:T(8,128)(2,1)} %shard_map.110), calls=%async_computation | async-start | bytes 1572864 | tf_op jit(solution)/shard_map/all_to_all | solution.py:275
  14.5 7.8 %shard_map.111.rc_ref = f32[576,128]{1,0:T(8,128)} custom-call(bf16[384,192,128]{2,1,0:T(8,128)(2,1)} %pg_hbm.5), custom_call_target="tpu_custom_call" | custom-call | flops 4831838208 | bytes 28311552 | tf_op jit(solution)/shard_map/pallas_call | solution.py:277
  22.3 8.4 %all-to-all-done.qk_ref = bf16[128,24,128]{2,1,0:T(8,128)(2,1)S(1)} async-done(((bf16[128,24,128]{2,1,0:T(8,128)(2,1)}), bf16[128,24,128]{2,1,0:T(8,128)(2,1)S(1)}, u32[]{:S(2)}, u32[]{:S(2)}) %all-to-all-start) | async-done | bytes 786464 | tf_op jit(solution)/shard_map/all_to_all | solution.py:275
  30.7 0.0 copy-done.5
  30.8 1.0 copy-done
  31.7 0.0 copy-start.2
  31.7 9.4 %shard_map.112 = (bf16[128,24,128]{2,1,0:T(8,128)(2,1)}, f32[1,128]{1,0:T(1,128)S(1)}) custom-call(bf16[128,24,128]{2,1,0:T(8,128)(2,1)S(1)} %all-to-all-done.qk_ref, f32[576,128]{1,0:T(8,128)S(1)} %copy-done, bf16[128,128]{1,0:T(8,128)(2,1)S(1)} %copy-done.5, bf16[384,192,128]{2,1,0:T(8,128)(2,1)} %pg_hbm.5), custom_call_target="tpu_custom_call" | custom-call | tf_op jit(solution)/shard_map/pallas_call | solution.py:289
  41.1 4.9 %all-to-all-start.1 = ((bf16[128,24,128]{2,1,0:T(8,128)(2,1)}), bf16[128,24,128]{2,1,0:T(8,128)(2,1)S(1)}, u32[]{:S(2)}, u32[]{:S(2)}) async-start(bf16[128,24,128]{2,1,0:T(8,128)(2,1)} %get-tuple-element.16), calls=%async_computation.1 | async-start | bytes 1572864 | tf_op jit(solution)/shard_map/all_to_all | solution.py:306
  46.0 0.0 copy-done.1
  46.0 7.4 %shard_map.113 = (f32[128,128]{1,0:T(8,128)S(1)}, f32[1,128]{1,0:T(1,128)S(1)}) custom-call(bf16[128,24,128]{2,1,0:T(8,128)(2,1)S(1)} %all-to-all-done.qk_ref, f32[576,128]{1,0:T(8,128)S(1)} %copy-done.1, bf16[384,192,128]{2,1,0:T(8,128)(2,1)} %pg_hbm.5), custom_call_target="tpu_custom_call" | custom-call | flops 4831838208 | bytes 18874368 | tf_op jit(solution)/shard_map/pallas_call | solution.py:308
  53.4 8.8 %all-to-all-done.1.dqk_ref = bf16[128,24,128]{2,1,0:T(8,128)(2,1)S(1)} async-done(((bf16[128,24,128]{2,1,0:T(8,128)(2,1)}), bf16[128,24,128]{2,1,0:T(8,128)(2,1)S(1)}, u32[]{:S(2)}, u32[]{:S(2)}) %all-to-all-start.1) | async-done | bytes 786464 | tf_op jit(solution)/shard_map/all_to_all | solution.py:306
  62.3 0.0 copy-done.3
  62.3 0.0 copy-done.4
  62.3 0.0 copy-done.6
  62.3 0.5 shard_map.114
  62.8 18.1 %all_to_all.20.x_ref = bf16[128,16,128]{2,1,0:T(8,128)(2,1)S(1)} all-to-all(bf16[128,16,128]{2,1,0:T(8,128)(2,1)S(1)} %get-tuple-element.21), channel_id=1, replica_groups=mesh['row'=8,'col'=16] {'row','col'}, dimensions={0} | all-to-all | bytes 1048576 | tf_op jit(solution)/shard_map/all_to_all | solution.py:332
  80.9 1.0 shard_map.116
  81.9 4.9 %all-to-all-start.3 = ((bf16[128,16,128]{2,1,0:T(8,128)(2,1)}), bf16[128,16,128]{2,1,0:T(8,128)(2,1)S(1)}, u32[]{:S(2)}, u32[]{:S(2)}) async-start(bf16[128,16,128]{2,1,0:T(8,128)(2,1)} %get-tuple-element.22), calls=%async_computation.3 | async-start | bytes 1048576 | tf_op jit(solution)/shard_map/all_to_all | solution.py:341
  86.8 0.0 copy-done.2
  86.8 0.9 shard_map.115
  87.7 12.5 %all-to-all-done.3.x_ref = bf16[128,16,128]{2,1,0:T(8,128)(2,1)S(1)} async-done(((bf16[128,16,128]{2,1,0:T(8,128)(2,1)}), bf16[128,16,128]{2,1,0:T(8,128)(2,1)S(1)}, u32[]{:S(2)}, u32[]{:S(2)}) %all-to-all-start.3) | async-done | bytes 524320 | tf_op jit(solution)/shard_map/all_to_all | solution.py:341
  100.2 0.9 shard_map.117
  (5 shorter events, 0.0 us)
Async XLA Ops:
  0.6 30.1 %copy-start.5 = (bf16[128,128]{1,0:T(8,128)(2,1)S(1)}, bf16[128,128]{1,0:T(8,128)(2,1)}, u32[]{:S(2)}) copy-start(bf16[128,128]{1,0:T(8,128)(2,1)} %w_hbm.3) | copy-start | bytes 98308
  3.0 27.8 %all-to-all-start = ((bf16[128,24,128]{2,1,0:T(8,128)(2,1)}), bf16[128,24,128]{2,1,0:T(8,128)(2,1)S(1)}, u32[]{:S(2)}, u32[]{:S(2)}) async-start(bf16[128,24,128]{2,1,0:T(8,128)(2,1)} %shard_map.110), calls=%async_computation | async-start | bytes 1572864 | tf_op jit(solution)/shard_map/all_to_all | solution.py:275
  30.8 1.0 copy-start
  31.7 14.3 %copy-start.1 = (f32[576,128]{1,0:T(8,128)S(1)}, f32[576,128]{1,0:T(8,128)}, u32[]{:S(2)}) copy-start(f32[576,128]{1,0:T(8,128)} %shard_map.111.rc_ref) | copy-start | bytes 884740
  31.7 30.5 %copy-start.3 = (bf16[24,1024]{1,0:T(8,128)(2,1)S(1)}, bf16[24,1024]{1,0:T(8,128)(2,1)}, u32[]{:S(2)}) copy-start(bf16[24,1024]{1,0:T(8,128)(2,1)} %seq_ref.3) | copy-start | bytes 147460
  31.7 30.5 %copy-start.4 = (f32[1024]{0:T(1024)S(1)}, f32[1024]{0:T(1024)}, u32[]{:S(2)}) copy-start(f32[1024]{0:T(1024)} %param.8) | copy-start | bytes 12292
  31.7 30.5 %copy-start.6 = (f32[1024]{0:T(1024)S(1)}, f32[1024]{0:T(1024)}, u32[]{:S(2)}) copy-start(f32[1024]{0:T(1024)} %param.9) | copy-start | bytes 12292
  31.7 55.1 %copy-start.2 = (bf16[1024,128]{1,0:T(8,128)(2,1)S(1)}, bf16[1024,128]{1,0:T(8,128)(2,1)}, u32[]{:S(2)}) copy-start(bf16[1024,128]{1,0:T(8,128)(2,1)} %w_ref.1) | copy-start | bytes 786436
  41.1 21.1 %all-to-all-start.1 = ((bf16[128,24,128]{2,1,0:T(8,128)(2,1)}), bf16[128,24,128]{2,1,0:T(8,128)(2,1)S(1)}, u32[]{:S(2)}, u32[]{:S(2)}) async-start(bf16[128,24,128]{2,1,0:T(8,128)(2,1)} %get-tuple-element.16), calls=%async_computation.1 | async-start | bytes 1572864 | tf_op jit(solution)/shard_map/all_to_all | solution.py:306
  81.9 18.3 %all-to-all-start.3 = ((bf16[128,16,128]{2,1,0:T(8,128)(2,1)}), bf16[128,16,128]{2,1,0:T(8,128)(2,1)S(1)}, u32[]{:S(2)}, u32[]{:S(2)}) async-start(bf16[128,16,128]{2,1,0:T(8,128)(2,1)} %get-tuple-element.22), calls=%async_computation.3 | async-start | bytes 1048576 | tf_op jit(solution)/shard_map/all_to_all | solution.py:341

commit v3 on v2

--- a/solution.py
+++ b/solution.py
@@ -56,7 +56,7 @@
     return copy
 
 
-def _totals_kernel(pg_hbm, rc_ref, pg, sems):
+def _totals_kernel(pg_hbm, rc_hbm, pg, sems, rc_ref, rc_sem):
     rows, cols, pair = pg.shape
     copy = _tile_copies(pg_hbm, pg, sems)
     over_i = pl.ds(rows, cols)
@@ -74,28 +74,48 @@
         return carry
 
     lax.fori_loop(0, rows // CHUNK, chunk, 0)
-
-
-def _own_qk(qk_ref, nq, nk):
-    shard, pair = qk_ref.shape[1:]
+    _fetch([(rc_ref, rc_hbm)], rc_sem)
+
+
+def _pack(x):
+    n, shard, inner = x.shape
+    x = x.reshape(n, shard // 8, 8, inner)
+    return jnp.concatenate([x[:, :, :4], x[:, :, 4:]], axis=3)
+
+
+def _unpack(x):
+    inner = x.shape[-1] // 2
+    x = jnp.concatenate([x[:, :, :inner], x[:, :, inner:]], axis=1)
+    return x.reshape(x.shape[0] * 8, inner)
+
+
+def _own_slots(qk_hbm, q_s, k_s):
+    nq, nk = q_s.shape[0], k_s.shape[0]
+    return [
+        (qk_hbm.at[pl.ds(lax.axis_index("row") * nq, nq)], q_s),
+        (qk_hbm.at[pl.ds(lax.axis_index("col") * nk, nk)], k_s),
+    ]
+
+
+def _own_qk(q_s, k_s):
+    nq, shard, pair = q_s.shape
     inner = pair // 2
-    me_r = lax.axis_index("row")
-    me_c = lax.axis_index("col")
-    q = qk_ref[pl.ds(me_r * nq, nq)].astype(F32).reshape(nq * shard, pair)[:, :inner]
-    k = qk_ref[pl.ds(me_c * nk, nk)].astype(F32).reshape(nk * shard, pair)[:, inner:]
+    q = q_s[...].astype(F32).reshape(nq * shard, pair)[:, :inner]
+    k = k_s[...].astype(F32).reshape(k_s.shape[0] * shard, pair)[:, inner:]
     return q, k
 
 
 def _sums_kernel(
-    nq, nk, qk_ref, rc_ref, w_hbm, pg_hbm, out_ref, bp_ref,
-    pg, sems, w_s, w_sem, wbd_s, q2_s, k2_s, dq_s, dk_s,
+    nq, nk, qk_hbm, rc_hbm, w_hbm, pg_hbm, seqk_hbm, out_ref, home_ref, bp_ref,
+    pg, sems, q_s, k_s, w_s, rc_s, in_sems, wbd_s, q2_s, k2_s, dq_s, dk_s, piece_s,
 ):
     rows, cols, pair = pg.shape
     inner, half = pair // 2, cols // 2
-    shard = out_ref.shape[1]
+    shard = home_ref.shape[0]
     copy = _tile_copies(pg_hbm, pg, sems)
-    _fetch([(w_hbm, w_s)], w_sem)
-    q, k = _own_qk(qk_ref, nq, nk)
+    del seqk_hbm
+    _fetch(_own_slots(qk_hbm, q_s, k_s) + [(w_hbm, w_s), (rc_hbm, rc_s)], in_sems)
+    q, k = _own_qk(q_s, k_s)
     q2_s[...] = jnp.concatenate([q, q], axis=1)
     k2_s[...] = jnp.concatenate([k[:half], k[half:]], axis=1)
     wt = w_s[...].astype(F32).T
@@ -104,7 +124,7 @@
     bottom = jnp.concatenate([blank, wt[:, :inner]], axis=1)
     wbd_s[...] = jnp.concatenate([top, bottom], axis=0).astype(BF16)
     gd = jnp.dot(
-        rc_ref[...], wt[:, inner:], precision=lax.Precision.HIGHEST, preferred_element_type=F32
+        rc_s[...], wt[:, inner:], precision=lax.Precision.HIGHEST, preferred_element_type=F32
     )
     dk_s[...] = jnp.zeros_like(dk_s)
     out_ref[...] = jnp.zeros_like(out_ref)
@@ -134,28 +154,32 @@
     bp_ref[...] = jnp.concatenate(
         [jnp.sum(dq, axis=0, keepdims=True), jnp.sum(dk, axis=0, keepdims=True)], axis=1
     )
-    dq = jnp.concatenate([dq, jnp.zeros_like(dq)], axis=1).reshape(nq, shard, pair)
-    dk = jnp.concatenate([jnp.zeros_like(dk), dk], axis=1).reshape(nk, shard, pair)
-    at_q = pl.ds(lax.axis_index("row") * nq, nq)
-    at_k = pl.ds(lax.axis_index("col") * nk, nk)
-    out_ref[at_q] = dq.astype(BF16)
-    out_ref[at_k] = (out_ref[at_k].astype(F32) + dk).astype(BF16)
+    me_r = lax.axis_index("row")
+    me_c = lax.axis_index("col")
+    dk = dk.reshape(nk, shard, inner)
+    piece_s[...] = dk
+    home_ref[...] = piece_s[me_r]
+    packed = _pack(dk).astype(BF16)
+    for m in range(nk):
+        out_ref[m * nq + me_c] = packed[m]
+    out_ref[pl.ds(me_r * nq, nq)] = _pack(dq.reshape(nq, shard, inner)).astype(BF16)
 
 
 def _weight_kernel(
-    nq, nk, qk_ref, rc_ref, pg_hbm, dw_ref, db_ref, pg, sems, qt_s, kt_s, dwp_s
+    qk_hbm, rc_hbm, pg_hbm, dw_ref, db_ref, pg, sems, q_s, k_s, rc_s, in_sems, qt_s, kt_s, dwp_s
 ):
     rows, cols, pair = pg.shape
     inner = pair // 2
     n_chunks = rows // CHUNK
     copy = _tile_copies(pg_hbm, pg, sems)
-    q, k = _own_qk(qk_ref, nq, nk)
+    _fetch(_own_slots(qk_hbm, q_s, k_s) + [(rc_hbm, rc_s)], in_sems)
+    q, k = _own_qk(q_s, k_s)
     qt, kt = q.T, k.T
     for ch in range(n_chunks):
         qt_s[ch] = qt[:, ch * CHUNK : (ch + 1) * CHUNK]
     kt_s[...] = kt.astype(BF16)
     dwp_s[...] = jnp.zeros_like(dwp_s)
-    rc = rc_ref[...]
+    rc = rc_s[...]
     dw_ref[inner:, :] = jnp.dot(
         jnp.concatenate([qt, -kt], axis=1),
         rc,
@@ -190,44 +214,58 @@
 
 
 def _grad_kernel(
-    seq_ref, gain_ref, beta_ref, dqk_ref, dw_ref, db_ref, bp_ref, out_ref, dqkb_ref
+    nq, nk, seq_ref, seqk_ref, gain_ref, beta_ref, dqk_ref, home_ref, dw_ref, db_ref, bp_ref,
+    out_ref, dqb_ref, dkb_ref,
 ):
-    dqk_b = jnp.sum(dqk_ref[...].astype(F32), axis=0).astype(BF16)
-    dqkb_ref[...] = dqk_b
-    y = (_norm(seq_ref[...])[0] * gain_ref[...] + beta_ref[...]).astype(BF16)
-    w_proj = lax.dot_general(y, dqk_b, (((0,), (0,)), ((), ())), preferred_element_type=F32)
-    n = out_ref.shape[0]
-    pair = out_ref.shape[2]
-    w_hi, w_lo = _split(dw_ref[...])
-    bo_hi, bo_lo = _split(db_ref[...])
+    me_r = lax.axis_index("row")
+    me_c = lax.axis_index("col")
+    dq = _unpack(jnp.sum(dqk_ref[pl.ds(me_r * nq, nq)].astype(F32), axis=0))
+    dk = home_ref[...]
+    for m in range(nk):
+        part = _unpack(dqk_ref[m * nq + me_c].astype(F32))
+        dk = dk + jnp.where(me_r == m, jnp.zeros_like(part), part)
+    dq_b, dk_b = dq.astype(BF16), dk.astype(BF16)
+    dqb_ref[...] = dq_b
+    dkb_ref[...] = dk_b
+    dims = (((0,), (0,)), ((), ()))
+
+    def rows_of(ref, cotangent):
+        y = (_norm(ref[...])[0] * gain_ref[...] + beta_ref[...]).astype(BF16)
+        return lax.dot_general(y, cotangent, dims, preferred_element_type=F32)
+
+    w_proj = jnp.concatenate([rows_of(seq_ref, dq_b), rows_of(seqk_ref, dk_b)], axis=1)
+    n, _, quarter, pair = out_ref.shape
+    w_proj = w_proj.reshape(n, 2 * quarter, pair)
+    out_ref[:, 0] = w_proj[:, :quarter].astype(BF16)
+    out_ref[:, 1] = w_proj[:, quarter:].astype(BF16)
     bp_hi, bp_lo = _split(bp_ref[...])
-    place = lax.broadcasted_iota(jnp.int32, (n, 8, pair), 1)
-    lower = jnp.zeros((n, 8, pair), F32)
-    for at, value in enumerate(
-        (w_hi[:, None, :], w_lo[:, None, :], bo_hi[None], bo_lo[None], bp_hi[None], bp_lo[None])
-    ):
-        lower = jnp.where(place == at, jnp.broadcast_to(value, lower.shape), lower)
-    out_ref[...] = jnp.concatenate([w_proj.reshape(n, 8, pair), lower], axis=1).astype(BF16)
+    place = lax.broadcasted_iota(jnp.int32, (n, quarter, pair), 1)
+    last = jnp.broadcast_to(dw_ref[...][:, None, :], place.shape)
+    for at, value in enumerate((db_ref[...], bp_hi, bp_lo), 1):
+        last = jnp.where(place == at, jnp.broadcast_to(value[None], place.shape), last)
+    out_ref[:, 2] = last.astype(BF16)
 
 
 def _reduce_kernel(x_ref, out_ref, bo_ref, bp_ref):
     total = jnp.sum(x_ref[...].astype(F32), axis=0)
-    bo_ref[...] = total[10:11] + total[11:12]
-    bp_ref[...] = total[12:13] + total[13:14]
-    w_hi, w_lo = _split(total[8:9] + total[9:10])
-    tile = jnp.concatenate([total[:8], w_hi, w_lo, jnp.zeros((6, total.shape[1]), F32)], axis=0)
-    out_ref[...] = jnp.broadcast_to(tile.astype(BF16)[None], out_ref.shape)
+    last = total[2]
+    bo_ref[...] = last[1:2]
+    bp_ref[...] = last[2:3] + last[3:4]
+    w_hi, w_lo = _split(last[0:1])
+    last = jnp.concatenate([w_hi, w_lo, jnp.zeros((2, last.shape[1]), F32)], axis=0)
+    tile = jnp.concatenate([total[:2], last[None]], axis=0).astype(BF16)
+    out_ref[...] = jnp.broadcast_to(tile[None], out_ref.shape)
 
 
 def _unpack_kernel(x_ref, w_proj_ref, w_out_ref):
     x = x_ref[...].astype(F32)
-    w_proj_ref[...] = x[:, :8].reshape(w_proj_ref.shape)
-    w_out_ref[...] = x[:, 8] + x[:, 9]
-
-
-def _seq_kernel(seq_ref, gain_ref, w_ref, dqk_ref, out_ref):
+    w_proj_ref[...] = jnp.concatenate([x[:, 0], x[:, 1]], axis=1).reshape(w_proj_ref.shape)
+    w_out_ref[...] = x[:, 2, 0] + x[:, 2, 1]
+
+
+def _seq_kernel(seq_ref, gain_ref, w_ref, dq_ref, dk_ref, out_ref):
     normed, inverse = _norm(seq_ref[...])
-    dqk = dqk_ref[...]
+    dqk = jnp.concatenate([dq_ref[...], dk_ref[...]], axis=1)
     dn = (
         lax.dot_general(dqk, w_ref[...], (((1,), (1,)), ((), ())), preferred_element_type=F32)
         * gain_ref[...]
@@ -272,46 +310,57 @@
         ],
         compiler_params=_params(60),
     )(seq, gain, beta, w_proj, b_proj.reshape(1, pair))
+    to_sum = [(d, (d % nk) * n_col + d // nk) for d in range(n)]
+    to_owner = [(b, a) for a, b in to_sum]
+    seq_k = lax.ppermute(seq, BOTH, to_sum)
     qk_all = lax.all_to_all(qk, BOTH, 0, 0, tiled=True)
 
     rc = pl.pallas_call(
         _totals_kernel,
         out_shape=shape((rows + cols, pair), F32),
         in_specs=[hbm],
-        out_specs=vmem,
-        scratch_shapes=tile,
+        out_specs=hbm,
+        scratch_shapes=tile + [pltpu.VMEM((rows + cols, pair), F32), pltpu.SemaphoreType.DMA((1,))],
         compiler_params=_params(60),
         cost_estimate=pl.CostEstimate(
             flops=4 * rows * cols * pair * pair, bytes_accessed=3 * rows * cols * pair, transcendentals=0
         ),
     )(pair_grad)
 
-    dqk_part, bp_part = pl.pallas_call(
+    own = [pltpu.VMEM((nq, shard, pair), BF16), pltpu.VMEM((nk, shard, pair), BF16)]
+    slot = shape((n, shard // 8, 4, pair), BF16)
+    dqk_part, home, bp_part = pl.pallas_call(
         functools.partial(_sums_kernel, nq, nk),
-        out_shape=(shape((n, shard, pair), BF16), shape((1, pair), F32)),
-        in_specs=[vmem, vmem, hbm, hbm],
-        out_specs=(vmem,) * 2,
+        out_shape=(slot, shape((shard, inner), F32), shape((1, pair), F32)),
+        in_specs=[hbm] * 5,
+        out_specs=(vmem,) * 3,
         scratch_shapes=tile
+        + own
         + [
             pltpu.VMEM((pair, pair), BF16),
-            pltpu.SemaphoreType.DMA((1,)),
+            pltpu.VMEM((rows + cols, pair), F32),
+            pltpu.SemaphoreType.DMA((4,)),
             pltpu.VMEM((2 * pair, pair), BF16),
             pltpu.VMEM((rows, pair), F32),
             pltpu.VMEM((cols // 2, pair), F32),
             pltpu.VMEM((rows, pair), F32),
             pltpu.VMEM((cols // 2, pair), F32),
+            pltpu.VMEM((nk, shard, inner), F32),
         ],
         compiler_params=_params(40),
-    )(qk_all, rc, w_out, pair_grad)
+    )(qk_all, rc, w_out, pair_grad, seq_k)
     dqk_in = lax.all_to_all(dqk_part, BOTH, 0, 0, tiled=True)
 
     dw_part, db_part = pl.pallas_call(
-        functools.partial(_weight_kernel, nq, nk),
+        _weight_kernel,
         out_shape=(shape((pair, pair), F32), shape((1, pair), F32)),
-        in_specs=[vmem, vmem, hbm],
+        in_specs=[hbm] * 3,
         out_specs=(vmem,) * 2,
         scratch_shapes=tile
+        + own
         + [
+            pltpu.VMEM((rows + cols, pair), F32),
+            pltpu.SemaphoreType.DMA((3,)),
             pltpu.VMEM((rows // CHUNK, inner, CHUNK), F32),
             pltpu.VMEM((inner, cols), BF16),
             pltpu.VMEM((inner, pair), F32),
@@ -322,18 +371,19 @@
         ),
     )(qk_all, rc, pair_grad)
 
-    slots, dqk_b = pl.pallas_call(
-        _grad_kernel,
-        out_shape=(shape((n, 16, pair), BF16), shape((shard, pair), BF16)),
-        in_specs=[vmem] * 7,
-        out_specs=(vmem,) * 2,
+    slots, dq_b, dk_b = pl.pallas_call(
+        functools.partial(_grad_kernel, nq, nk),
+        out_shape=(slot, shape((shard, inner), BF16), shape((shard, inner), BF16)),
+        in_specs=[vmem] * 9,
+        out_specs=(vmem,) * 3,
         compiler_params=_params(32),
-    )(seq, gain, beta, dqk_in, dw_part, db_part, bp_part)
+    )(seq, seq_k, gain, beta, dqk_in, home, dw_part, db_part, bp_part)
     gathered = lax.all_to_all(slots, BOTH, 0, 0, tiled=True)
+    dk_own = lax.ppermute(dk_b, BOTH, to_owner)
 
     reduced, d_b_out, d_b_proj = pl.pallas_call(
         _reduce_kernel,
-        out_shape=(shape((n, 16, pair), BF16), shape((1, pair), F32), shape((1, pair), F32)),
+        out_shape=(slot, shape((1, pair), F32), shape((1, pair), F32)),
         in_specs=[vmem],
         out_specs=(vmem,) * 3,
         compiler_params=_params(32),
@@ -343,10 +393,10 @@
     d_seq = pl.pallas_call(
         _seq_kernel,
         out_shape=shape(seq.shape, BF16),
-        in_specs=[vmem] * 4,
+        in_specs=[vmem] * 5,
         out_specs=vmem,
         compiler_params=_params(32),
-    )(seq, gain, w_proj, dqk_b)
+    )(seq, gain, w_proj, dq_b, dk_own)
 
     d_w_proj, d_w_out = pl.pallas_call(
         _unpack_kernel,

time: 101 us -> 95.7 us (0.948)
  waiting for transfers between devices: 29.7 us -> 15.6 us
  starting transfers between devices: 21.3 us -> 31.2 us
  blocking collectives: 18.1 us -> 16.8 us
    ppermute x0 -> x2, starting transfers between devices: none -> 8.72 us  [the longest x1 5.05 us: local(): dk_own = lax.ppermute(dk_b, BOTH, to_owner)]
    all_to_all x1, waiting for transfers between devices: 12.5 us -> 5.3 us  [local(): spread = lax.all_to_all(reduced, BOTH, 0, 0, tiled=True)]
    all_to_all x1, waiting for transfers between devices: 8.81 us -> 4.86 us  [local(): dqk_in = lax.all_to_all(dqk_part, BOTH, 0, 0, tiled=True)]
    all_to_all x1, waiting for transfers between devices: 8.42 us -> 4.7 us  [local(): qk_all = lax.all_to_all(qk, BOTH, 0, 0, tiled=True)]
    all_to_all x1, blocking collectives: 18.1 us -> 16.8 us  [local(): gathered = lax.all_to_all(slots, BOTH, 0, 0, tiled=True)]
    all_to_all x1, starting transfers between devices: 4.89 us -> 6.1 us  [local(): dqk_in = lax.all_to_all(dqk_part, BOTH, 0, 0, tiled=True)]
  transfers between devices with their start and end apart: 3 -> 5, of which waited for: 3 -> 4; matrix products, arithmetic and copies ran while one was open for 0% -> 0% of each run, Pallas kernels for 16% -> 17%
where the time goes in v3:
time: 95.7 us; the launch traced here: 95.3 us
  starting transfers between devices  31.2 us (33%)
  Pallas kernels  30 us (31%)
  blocking collectives  16.8 us (18%)
  waiting for transfers between devices  15.6 us (16%)
  local copies, waits for them, and re-layouts  1 us (1%)
    all_to_all x1, blocking collectives, local(): gathered = lax.all_to_all(slots, BOTH, 0, 0, tiled=True)  16.8 us
    all_to_all x1, starting transfers between devices, local(): qk_all = lax.all_to_all(qk, BOTH, 0, 0, tiled=True)  11.5 us
    pallas_call x1, Pallas kernels, local(): pl.pallas_call(functools.partial(_sums_kernel, nq, nk), out_shape=(slot,...  9.06 us
    pallas_call x1, Pallas kernels, local(): pl.pallas_call(_totals_kernel, out_shape=shape((rows + cols, pair), F32),...  7.8 us
    pallas_call x1, Pallas kernels, local(): pl.pallas_call(_weight_kernel, out_shape=(shape((pair, pair), F32), shape...  7.18 us
    all_to_all x1, starting transfers between devices, local(): dqk_in = lax.all_to_all(dqk_part, BOTH, 0, 0, tiled=True)  6.1 us
    all_to_all x1, waiting for transfers between devices, local(): spread = lax.all_to_all(reduced, BOTH, 0, 0, tiled=True)  5.3 us
    ppermute x1, starting transfers between devices, local(): dk_own = lax.ppermute(dk_b, BOTH, to_owner)  5.05 us
  transfers between devices with their start and end apart: 5, of which 4 were waited for; matrix products, arithmetic and copies ran while one was open for 0% of the time, Pallas kernels for 17%

profile of v3, /device:TPU:1, one launch (start us, length us, event | category | flops | bytes accessed | tf_op | source)
XLA Modules:
  0.0 95.3 jit_solution(9569581774977888042)
XLA Ops:
  0.6 2.3 %shard_map.110 = bf16[128,24,128]{2,1,0:T(8,128)(2,1)} custom-call(bf16[24,1024]{1,0:T(8,128)(2,1)} %seq_ref.3, f32[1,1024]{1,0:T(1,128)} %bitcast.5, f32[1,1024]{1,0:T(1,128)} %bitcast.8, bf16[1024,128]{1,0:T(8,128)(2,1)} %w_ref.1, f32[1,128]{1,0:T(1,128)} %bitcast.10), custom_call_target="tpu_custom_call" | custom-call | tf_op jit(solution)/shard_map/pallas_call | solution.py:298
  3.0 11.5 %all-to-all-start = ((bf16[128,24,128]{2,1,0:T(8,128)(2,1)}), bf16[128,24,128]{2,1,0:T(8,128)(2,1)S(1)}, u32[]{:S(2)}, u32[]{:S(2)}) async-start(bf16[128,24,128]{2,1,0:T(8,128)(2,1)} %shard_map.110), calls=%async_computation | async-start | bytes 1572864 | tf_op jit(solution)/shard_map/all_to_all | solution.py:316
  14.5 3.7 %collective-permute-start = (bf16[24,1024]{1,0:T(8,128)(2,1)}, bf16[24,1024]{1,0:T(8,128)(2,1)S(1)}, u32[]{:S(2)}, u32[]{:S(2)}) collective-permute-start(bf16[24,1024]{1,0:T(8,128)(2,1)} %seq_ref.3), channel_id=1, source_target_pairs={{0,0},{1,16},{2,32},{3,48},{4,64},{5,80},{6,96},{7,112},{8,1},{9,1... | collective-permute-start | bytes 147464 | tf_op jit(solution)/shard_map/ppermute | solution.py:315
  18.2 0.0 copy-start.3
  18.2 0.0 copy-start.4
  18.2 0.0 copy-start.6
  18.2 0.0 copy-start.2
  18.2 7.8 %shard_map.111.rc_hbm = f32[576,128]{1,0:T(8,128)} custom-call(bf16[384,192,128]{2,1,0:T(8,128)(2,1)} %pg_hbm.5), custom_call_target="tpu_custom_call" | custom-call | flops 4831838208 | bytes 28311552 | tf_op jit(solution)/shard_map/pallas_call | solution.py:318
  26.0 0.0 collective-permute-done.seqk_hbm.seqk_ref
  26.0 4.7 %all-to-all-done.qk_hbm = bf16[128,24,128]{2,1,0:T(8,128)(2,1)S(1)} async-done(((bf16[128,24,128]{2,1,0:T(8,128)(2,1)}), bf16[128,24,128]{2,1,0:T(8,128)(2,1)S(1)}, u32[]{:S(2)}, u32[]{:S(2)}) %all-to-all-start) | async-done | bytes 786464 | tf_op jit(solution)/shard_map/all_to_all | solution.py:316
  30.7 1.0 %copy-done = f32[576,128]{1,0:T(8,128)S(1)} copy-done((f32[576,128]{1,0:T(8,128)S(1)}, f32[576,128]{1,0:T(8,128)}, u32[]{:S(2)}) %copy-start) | copy-done | bytes 294936
  31.7 9.1 %shard_map.112 = (bf16[128,3,4,128]{3,2,1,0:T(4,128)(2,1)}, f32[24,64]{1,0:T(8,128)S(1)}, f32[1,128]{1,0:T(1,128)S(1)}) custom-call(bf16[128,24,128]{2,1,0:T(8,128)(2,1)S(1)} %all-to-all-done.qk_hbm, f32[576,128]{1,0:T(8,128)S(1)} %copy-done, bf16[128,128]{1,0:T(8,128)(2,1)S(1)} %copy-done.5, bf16[384,192,128]{2,1,0:T(8,128)(2,1)} %pg_hbm.5, ...), custom_call_target="tpu_custom_call" | custom-call | tf_op jit(solution)/shard_map/pallas_call | solution.py:332
  40.8 6.1 %all-to-all-start.1 = ((bf16[128,3,4,128]{3,2,1,0:T(4,128)(2,1)}), bf16[128,3,4,128]{3,2,1,0:T(4,128)(2,1)S(1)}, u32[]{:S(2)}, u32[]{:S(2)}) async-start(bf16[128,3,4,128]{3,2,1,0:T(4,128)(2,1)} %get-tuple-element.18), calls=%async_computation.1 | async-start | bytes 786432 | tf_op jit(solution)/shard_map/all_to_all | solution.py:352
  46.9 7.2 %shard_map.113 = (f32[128,128]{1,0:T(8,128)S(1)}, f32[1,128]{1,0:T(1,128)S(1)}) custom-call(bf16[128,24,128]{2,1,0:T(8,128)(2,1)S(1)} %all-to-all-done.qk_hbm, f32[576,128]{1,0:T(8,128)S(1)} %copy-done.1, bf16[384,192,128]{2,1,0:T(8,128)(2,1)} %pg_hbm.5), custom_call_target="tpu_custom_call" | custom-call | flops 4831838208 | bytes 18874368 | tf_op jit(solution)/shard_map/pallas_call | solution.py:354
  54.1 4.9 %all-to-all-done.1.dqk_ref = bf16[128,3,4,128]{3,2,1,0:T(4,128)(2,1)S(1)} async-done(((bf16[128,3,4,128]{3,2,1,0:T(4,128)(2,1)}), bf16[128,3,4,128]{3,2,1,0:T(4,128)(2,1)S(1)}, u32[]{:S(2)}, u32[]{:S(2)}) %all-to-all-start.1) | async-done | bytes 393248 | tf_op jit(solution)/shard_map/all_to_all | solution.py:352
  59.0 0.7 shard_map.114
  59.7 16.8 %all_to_all.20.x_ref = bf16[128,3,4,128]{3,2,1,0:T(4,128)(2,1)S(1)} all-to-all(bf16[128,3,4,128]{3,2,1,0:T(4,128)(2,1)S(1)} %get-tuple-element.25), channel_id=1, replica_groups=mesh['row'=8,'col'=16] {'row','col'}, dimensions={0} | all-to-all | bytes 786432 | tf_op jit(solution)/shard_map/all_to_all | solution.py:381
  76.5 1.0 %shard_map.116 = (bf16[128,3,4,128]{3,2,1,0:T(4,128)(2,1)}, f32[1,128]{1,0:T(1,128)}, f32[1,128]{1,0:T(1,128)}) custom-call(bf16[128,3,4,128]{3,2,1,0:T(4,128)(2,1)S(1)} %all_to_all.20.x_ref), custom_call_target="tpu_custom_call" | custom-call | tf_op jit(solution)/shard_map/pallas_call | solution.py:384
  77.5 4.8 %all-to-all-start.3 = ((bf16[128,3,4,128]{3,2,1,0:T(4,128)(2,1)}), bf16[128,3,4,128]{3,2,1,0:T(4,128)(2,1)S(1)}, u32[]{:S(2)}, u32[]{:S(2)}) async-start(bf16[128,3,4,128]{3,2,1,0:T(4,128)(2,1)} %get-tuple-element.26), calls=%async_computation.3 | async-start | bytes 786432 | tf_op jit(solution)/shard_map/all_to_all | solution.py:391
  82.4 5.1 %collective-permute-start.1 = (bf16[24,64]{1,0:T(8,128)(2,1)S(1)}, bf16[24,64]{1,0:T(8,128)(2,1)S(1)}, u32[]{:S(2)}, u32[]{:S(2)}) collective-permute-start(bf16[24,64]{1,0:T(8,128)(2,1)S(1)} %get-tuple-element.24), channel_id=1, source_target_pairs={{0,0},{16,1},{32,2},{48,3},{64,4},{80,5},{96,6},{112,7},{1,8},{17,... | collective-permute-start | bytes 9224 | tf_op jit(solution)/shard_map/ppermute | solution.py:382
  87.4 0.8 collective-permute-done.1.dk_ref
  88.2 0.9 shard_map.115
  89.1 5.3 %all-to-all-done.3.x_ref = bf16[128,3,4,128]{3,2,1,0:T(4,128)(2,1)S(1)} async-done(((bf16[128,3,4,128]{3,2,1,0:T(4,128)(2,1)}), bf16[128,3,4,128]{3,2,1,0:T(4,128)(2,1)S(1)}, u32[]{:S(2)}, u32[]{:S(2)}) %all-to-all-start.3) | async-done | bytes 393248 | tf_op jit(solution)/shard_map/all_to_all | solution.py:391
  94.4 0.9 shard_map.117
  (9 shorter events, 0.0 us)
Async XLA Ops:
  0.6 30.1 %copy-start.5 = (bf16[128,128]{1,0:T(8,128)(2,1)S(1)}, bf16[128,128]{1,0:T(8,128)(2,1)}, u32[]{:S(2)}) copy-start(bf16[128,128]{1,0:T(8,128)(2,1)} %w_hbm.3) | copy-start | bytes 98308
  3.0 27.8 %all-to-all-start = ((bf16[128,24,128]{2,1,0:T(8,128)(2,1)}), bf16[128,24,128]{2,1,0:T(8,128)(2,1)S(1)}, u32[]{:S(2)}, u32[]{:S(2)}) async-start(bf16[128,24,128]{2,1,0:T(8,128)(2,1)} %shard_map.110), calls=%async_computation | async-start | bytes 1572864 | tf_op jit(solution)/shard_map/all_to_all | solution.py:316
  14.5 11.5 %collective-permute-start = (bf16[24,1024]{1,0:T(8,128)(2,1)}, bf16[24,1024]{1,0:T(8,128)(2,1)S(1)}, u32[]{:S(2)}, u32[]{:S(2)}) collective-permute-start(bf16[24,1024]{1,0:T(8,128)(2,1)} %seq_ref.3), channel_id=1, source_target_pairs={{0,0},{1,16},{2,32},{3,48},{4,64},{5,80},{6,96},{7,112},{8,1},{9,1... | collective-permute-start | bytes 147464 | tf_op jit(solution)/shard_map/ppermute | solution.py:315
  18.2 40.8 %copy-start.3 = (bf16[24,1024]{1,0:T(8,128)(2,1)S(1)}, bf16[24,1024]{1,0:T(8,128)(2,1)}, u32[]{:S(2)}) copy-start(bf16[24,1024]{1,0:T(8,128)(2,1)} %seq_ref.3) | copy-start | bytes 147460
  18.2 40.8 %copy-start.4 = (f32[1024]{0:T(1024)S(1)}, f32[1024]{0:T(1024)}, u32[]{:S(2)}) copy-start(f32[1024]{0:T(1024)} %param.8) | copy-start | bytes 12292
  18.2 40.8 %copy-start.6 = (f32[1024]{0:T(1024)S(1)}, f32[1024]{0:T(1024)}, u32[]{:S(2)}) copy-start(f32[1024]{0:T(1024)} %param.9) | copy-start | bytes 12292
  18.2 70.0 %copy-start.2 = (bf16[1024,128]{1,0:T(8,128)(2,1)S(1)}, bf16[1024,128]{1,0:T(8,128)(2,1)}, u32[]{:S(2)}) copy-start(bf16[1024,128]{1,0:T(8,128)(2,1)} %w_ref.1) | copy-start | bytes 786436
  30.7 1.0 %copy-start = (f32[576,128]{1,0:T(8,128)S(1)}, f32[576,128]{1,0:T(8,128)}, u32[]{:S(2)}) copy-start(f32[576,128]{1,0:T(8,128)} %shard_map.111.rc_hbm) | copy-start | bytes 884740
  31.7 15.2 %copy-start.1 = (f32[576,128]{1,0:T(8,128)S(1)}, f32[576,128]{1,0:T(8,128)}, u32[]{:S(2)}) copy-start(f32[576,128]{1,0:T(8,128)} %shard_map.111.rc_hbm) | copy-start | bytes 884740
  40.8 18.2 %all-to-all-start.1 = ((bf16[128,3,4,128]{3,2,1,0:T(4,128)(2,1)}), bf16[128,3,4,128]{3,2,1,0:T(4,128)(2,1)S(1)}, u32[]{:S(2)}, u32[]{:S(2)}) async-start(bf16[128,3,4,128]{3,2,1,0:T(4,128)(2,1)} %get-tuple-element.18), calls=%async_computation.1 | async-start | bytes 786432 | tf_op jit(solution)/shard_map/all_to_all | solution.py:352
  77.5 16.9 %all-to-all-start.3 = ((bf16[128,3,4,128]{3,2,1,0:T(4,128)(2,1)}), bf16[128,3,4,128]{3,2,1,0:T(4,128)(2,1)S(1)}, u32[]{:S(2)}, u32[]{:S(2)}) async-start(bf16[128,3,4,128]{3,2,1,0:T(4,128)(2,1)} %get-tuple-element.26), calls=%async_computation.3 | async-start | bytes 786432 | tf_op jit(solution)/shard_map/all_to_all | solution.py:391
  82.4 5.8 %collective-permute-start.1 = (bf16[24,64]{1,0:T(8,128)(2,1)S(1)}, bf16[24,64]{1,0:T(8,128)(2,1)S(1)}, u32[]{:S(2)}, u32[]{:S(2)}) collective-permute-start(bf16[24,64]{1,0:T(8,128)(2,1)S(1)} %get-tuple-element.24), channel_id=1, source_target_pairs={{0,0},{16,1},{32,2},{48,3},{64,4},{80,5},{96,6},{112,7},{1,8},{17,... | collective-permute-start | bytes 9224 | tf_op jit(solution)/shard_map/ppermute | solution.py:382

commit v4 on v3

--- a/solution.py
+++ b/solution.py
@@ -10,7 +10,7 @@
 F32 = jnp.float32
 BF16 = jnp.bfloat16
 BOTH = ("row", "col")
-CHUNK = 48
+CHUNK = 64
 
 
 def _params(mib):
@@ -25,25 +25,40 @@
     return centred * inverse, inverse
 
 
-def _fetch(pairs, sems):
+def _start(pairs, sems):
     copies = [pltpu.make_async_copy(a, b, sems.at[n]) for n, (a, b) in enumerate(pairs)]
     for c in copies:
         c.start()
-    for c in copies:
+    return copies
+
+
+def _fetch(pairs, sems):
+    for c in _start(pairs, sems):
         c.wait()
 
 
+def _spread(block_s, out_hbm, sems):
+    count = block_s.shape[0]
+    parts = range(0, out_hbm.shape[0], count)
+    _fetch([(block_s, out_hbm.at[pl.ds(at, count)]) for at in parts], sems)
+
+
 def _project_kernel(
-    seq_hbm, gain_hbm, beta_hbm, w_hbm, b_hbm, out_ref, seq_s, gain_s, beta_s, w_s, b_s, sems
+    seq_hbm, gain_hbm, beta_hbm, w_hbm, b_hbm, out_hbm,
+    seq_s, gain_s, beta_s, w_s, b_s, sems, block_s, out_sems,
 ):
-    _fetch(
+    copies = _start(
         [(seq_hbm, seq_s), (gain_hbm, gain_s), (beta_hbm, beta_s), (w_hbm, w_s), (b_hbm, b_s)],
         sems,
     )
+    copies[0].wait()
     normed, _ = _norm(seq_s[...])
+    for c in copies[1:]:
+        c.wait()
     y = (normed * gain_s[...] + beta_s[...]).astype(BF16)
     qk = (jnp.dot(y, w_s[...], preferred_element_type=F32) + b_s[...]).astype(BF16)
-    out_ref[...] = jnp.broadcast_to(qk[None], out_ref.shape)
+    block_s[...] = jnp.broadcast_to(qk[None], block_s.shape)
+    _spread(block_s, out_hbm, out_sems)
 
 
 def _tile_copies(pg_hbm, pg, sems):
@@ -112,9 +127,11 @@
     rows, cols, pair = pg.shape
     inner, half = pair // 2, cols // 2
     shard = home_ref.shape[0]
+    del seqk_hbm
+    small = _start(_own_slots(qk_hbm, q_s, k_s) + [(w_hbm, w_s), (rc_hbm, rc_s)], in_sems)
     copy = _tile_copies(pg_hbm, pg, sems)
-    del seqk_hbm
-    _fetch(_own_slots(qk_hbm, q_s, k_s) + [(w_hbm, w_s), (rc_hbm, rc_s)], in_sems)
+    for c in small[:3]:
+        c.wait()
     q, k = _own_qk(q_s, k_s)
     q2_s[...] = jnp.concatenate([q, q], axis=1)
     k2_s[...] = jnp.concatenate([k[:half], k[half:]], axis=1)
@@ -123,9 +140,6 @@
     top = jnp.concatenate([wt[:, :inner], blank], axis=1)
     bottom = jnp.concatenate([blank, wt[:, :inner]], axis=1)
     wbd_s[...] = jnp.concatenate([top, bottom], axis=0).astype(BF16)
-    gd = jnp.dot(
-        rc_s[...], wt[:, inner:], precision=lax.Precision.HIGHEST, preferred_element_type=F32
-    )
     dk_s[...] = jnp.zeros_like(dk_s)
     out_ref[...] = jnp.zeros_like(out_ref)
 
@@ -147,6 +161,10 @@
         return carry
 
     lax.fori_loop(0, rows // CHUNK, chunk, 0)
+    small[3].wait()
+    gd = jnp.dot(
+        rc_s[...], w_s[...].astype(F32).T[:, inner:], precision=lax.Precision.HIGHEST, preferred_element_type=F32
+    )
     dq = dq_s[...]
     dq = dq[:, :inner] + dq[:, inner:] + gd[:rows]
     dk = dk_s[...]
@@ -299,7 +317,7 @@
         _project_kernel,
         out_shape=shape((n, shard, pair), BF16),
         in_specs=[hbm] * 5,
-        out_specs=vmem,
+        out_specs=hbm,
         scratch_shapes=[
             pltpu.VMEM((shard, width), BF16),
             pltpu.VMEM((1, width), F32),
@@ -307,6 +325,8 @@
             pltpu.VMEM((width, pair), BF16),
             pltpu.VMEM((1, pair), F32),
             pltpu.SemaphoreType.DMA((5,)),
+            pltpu.VMEM((n // 8, shard, pair), BF16),
+            pltpu.SemaphoreType.DMA((8,)),
         ],
         compiler_params=_params(60),
     )(seq, gain, beta, w_proj, b_proj.reshape(1, pair))
@@ -348,7 +368,7 @@
             pltpu.VMEM((nk, shard, inner), F32),
         ],
         compiler_params=_params(40),
-    )(qk_all, rc, w_out, pair_grad, seq_k)
+    )(qk_all, pltpu.with_memory_space_constraint(rc, pltpu.HBM), w_out, pair_grad, seq_k)
     dqk_in = lax.all_to_all(dqk_part, BOTH, 0, 0, tiled=True)
 
     dw_part, db_part = pl.pallas_call(

time: 95.7 us -> 95 us (level)
  local copies, waits for them, and re-layouts: 1 us -> 0.03 us
    unnamed x14 -> x12, local copies, waits for them, and re-layouts: 1 us -> 0.03 us
where the time goes in v4:
time: 95 us; the launch traced here: 94.6 us
  starting transfers between devices  31.2 us (33%)
  Pallas kernels  30.3 us (32%)
  blocking collectives  16.9 us (18%)
  waiting for transfers between devices  15.4 us (16%)
    all_to_all x1, blocking collectives, local(): gathered = lax.all_to_all(slots, BOTH, 0, 0, tiled=True)  16.9 us
    all_to_all x1, starting transfers between devices, local(): qk_all = lax.all_to_all(qk, BOTH, 0, 0, tiled=True)  11.5 us
    pallas_call x1, Pallas kernels, local(): pl.pallas_call(functools.partial(_sums_kernel, nq, nk), out_shape=(slot,...  9.32 us
    pallas_call x1, Pallas kernels, local(): pl.pallas_call(_totals_kernel, out_shape=shape((rows + cols, pair), F32),...  7.91 us
    pallas_call x1, Pallas kernels, local(): pl.pallas_call(_weight_kernel, out_shape=(shape((pair, pair), F32), shape...  7.31 us
    all_to_all x1, starting transfers between devices, local(): dqk_in = lax.all_to_all(dqk_part, BOTH, 0, 0, tiled=True)  6.11 us
    all_to_all x1, waiting for transfers between devices, local(): spread = lax.all_to_all(reduced, BOTH, 0, 0, tiled=True)  5.3 us
    ppermute x1, starting transfers between devices, local(): dk_own = lax.ppermute(dk_b, BOTH, to_owner)  5.05 us
  transfers between devices with their start and end apart: 5, of which 4 were waited for; matrix products, arithmetic and copies ran while one was open for 0% of the time, Pallas kernels for 17%

profile of v4, /device:TPU:1, one launch (start us, length us, event | category | flops | bytes accessed | tf_op | source)
XLA Modules:
  0.0 94.6 jit_solution(6018850839251131084)
XLA Ops:
  0.6 2.2 %shard_map.110 = bf16[128,24,128]{2,1,0:T(8,128)(2,1)} custom-call(bf16[24,1024]{1,0:T(8,128)(2,1)} %seq_ref.3, f32[1,1024]{1,0:T(1,128)} %bitcast.5, f32[1,1024]{1,0:T(1,128)} %bitcast.8, bf16[1024,128]{1,0:T(8,128)(2,1)} %w_ref.1, f32[1,128]{1,0:T(1,128)} %bitcast.10), custom_call_target="tpu_custom_call" | custom-call | tf_op jit(solution)/shard_map/pallas_call | solution.py:316
  2.8 11.5 %all-to-all-start = ((bf16[128,24,128]{2,1,0:T(8,128)(2,1)}), bf16[128,24,128]{2,1,0:T(8,128)(2,1)S(1)}, u32[]{:S(2)}, u32[]{:S(2)}) async-start(bf16[128,24,128]{2,1,0:T(8,128)(2,1)} %shard_map.110), calls=%async_computation | async-start | bytes 1572864 | tf_op jit(solution)/shard_map/all_to_all | solution.py:336
  14.4 3.7 %collective-permute-start = (bf16[24,1024]{1,0:T(8,128)(2,1)}, bf16[24,1024]{1,0:T(8,128)(2,1)S(1)}, u32[]{:S(2)}, u32[]{:S(2)}) collective-permute-start(bf16[24,1024]{1,0:T(8,128)(2,1)} %seq_ref.3), channel_id=1, source_target_pairs={{0,0},{1,16},{2,32},{3,48},{4,64},{5,80},{6,96},{7,112},{8,1},{9,1... | collective-permute-start | bytes 147464 | tf_op jit(solution)/shard_map/ppermute | solution.py:335
  18.0 7.9 %shard_map.111.rc_hbm = f32[576,128]{1,0:T(8,128)} custom-call(bf16[384,192,128]{2,1,0:T(8,128)(2,1)} %pg_hbm.5), custom_call_target="tpu_custom_call" | custom-call | flops 4831838208 | bytes 28311552 | tf_op jit(solution)/shard_map/pallas_call | solution.py:338
  26.0 0.0 copy-start.2
  26.0 0.0 copy-start.3
  26.0 0.0 copy-start.5
  26.0 0.0 copy-start.1
  26.0 0.0 collective-permute-done.seqk_hbm.seqk_ref
  26.0 4.6 %all-to-all-done.qk_hbm = bf16[128,24,128]{2,1,0:T(8,128)(2,1)S(1)} async-done(((bf16[128,24,128]{2,1,0:T(8,128)(2,1)}), bf16[128,24,128]{2,1,0:T(8,128)(2,1)S(1)}, u32[]{:S(2)}, u32[]{:S(2)}) %all-to-all-start) | async-done | bytes 786464 | tf_op jit(solution)/shard_map/all_to_all | solution.py:336
  30.6 0.0 copy-done.4
  30.6 9.3 %shard_map.112 = (bf16[128,3,4,128]{3,2,1,0:T(4,128)(2,1)}, f32[24,64]{1,0:T(8,128)S(1)}, f32[1,128]{1,0:T(1,128)S(1)}) custom-call(bf16[128,24,128]{2,1,0:T(8,128)(2,1)S(1)} %all-to-all-done.qk_hbm, f32[576,128]{1,0:T(8,128)} %shard_map.111.rc_hbm, bf16[128,128]{1,0:T(8,128)(2,1)S(1)} %copy-done.4, bf16[384,192,128]{2,1,0:T(8,128)(2,1)} %pg_hbm.5, ...), custom_call_target="tpu_custom_call" | custom-call | tf_op jit(solution)/shard_map/pallas_call | solution.py:352
  39.9 6.1 %all-to-all-start.1 = ((bf16[128,3,4,128]{3,2,1,0:T(4,128)(2,1)}), bf16[128,3,4,128]{3,2,1,0:T(4,128)(2,1)S(1)}, u32[]{:S(2)}, u32[]{:S(2)}) async-start(bf16[128,3,4,128]{3,2,1,0:T(4,128)(2,1)} %get-tuple-element.18), calls=%async_computation.1 | async-start | bytes 786432 | tf_op jit(solution)/shard_map/all_to_all | solution.py:372
  46.1 7.3 %shard_map.113 = (f32[128,128]{1,0:T(8,128)S(1)}, f32[1,128]{1,0:T(1,128)S(1)}) custom-call(bf16[128,24,128]{2,1,0:T(8,128)(2,1)S(1)} %all-to-all-done.qk_hbm, f32[576,128]{1,0:T(8,128)S(1)} %copy-done, bf16[384,192,128]{2,1,0:T(8,128)(2,1)} %pg_hbm.5), custom_call_target="tpu_custom_call" | custom-call | flops 4831838208 | bytes 18874368 | tf_op jit(solution)/shard_map/pallas_call | solution.py:374
  53.4 4.7 %all-to-all-done.1.dqk_ref = bf16[128,3,4,128]{3,2,1,0:T(4,128)(2,1)S(1)} async-done(((bf16[128,3,4,128]{3,2,1,0:T(4,128)(2,1)}), bf16[128,3,4,128]{3,2,1,0:T(4,128)(2,1)S(1)}, u32[]{:S(2)}, u32[]{:S(2)}) %all-to-all-start.1) | async-done | bytes 393248 | tf_op jit(solution)/shard_map/all_to_all | solution.py:372
  58.1 0.7 shard_map.114
  58.9 16.9 %all_to_all.20.x_ref = bf16[128,3,4,128]{3,2,1,0:T(4,128)(2,1)S(1)} all-to-all(bf16[128,3,4,128]{3,2,1,0:T(4,128)(2,1)S(1)} %get-tuple-element.25), channel_id=1, replica_groups=mesh['row'=8,'col'=16] {'row','col'}, dimensions={0} | all-to-all | bytes 786432 | tf_op jit(solution)/shard_map/all_to_all | solution.py:401
  75.8 1.0 %shard_map.116 = (bf16[128,3,4,128]{3,2,1,0:T(4,128)(2,1)}, f32[1,128]{1,0:T(1,128)}, f32[1,128]{1,0:T(1,128)}) custom-call(bf16[128,3,4,128]{3,2,1,0:T(4,128)(2,1)S(1)} %all_to_all.20.x_ref), custom_call_target="tpu_custom_call" | custom-call | tf_op jit(solution)/shard_map/pallas_call | solution.py:404
  76.8 4.8 %all-to-all-start.3 = ((bf16[128,3,4,128]{3,2,1,0:T(4,128)(2,1)}), bf16[128,3,4,128]{3,2,1,0:T(4,128)(2,1)S(1)}, u32[]{:S(2)}, u32[]{:S(2)}) async-start(bf16[128,3,4,128]{3,2,1,0:T(4,128)(2,1)} %get-tuple-element.26), calls=%async_computation.3 | async-start | bytes 786432 | tf_op jit(solution)/shard_map/all_to_all | solution.py:411
  81.7 5.1 %collective-permute-start.1 = (bf16[24,64]{1,0:T(8,128)(2,1)S(1)}, bf16[24,64]{1,0:T(8,128)(2,1)S(1)}, u32[]{:S(2)}, u32[]{:S(2)}) collective-permute-start(bf16[24,64]{1,0:T(8,128)(2,1)S(1)} %get-tuple-element.24), channel_id=1, source_target_pairs={{0,0},{16,1},{32,2},{48,3},{64,4},{80,5},{96,6},{112,7},{1,8},{17,... | collective-permute-start | bytes 9224 | tf_op jit(solution)/shard_map/ppermute | solution.py:402
  86.7 0.8 collective-permute-done.1.dk_ref
  87.5 0.9 shard_map.115
  88.4 5.3 %all-to-all-done.3.x_ref = bf16[128,3,4,128]{3,2,1,0:T(4,128)(2,1)S(1)} async-done(((bf16[128,3,4,128]{3,2,1,0:T(4,128)(2,1)}), bf16[128,3,4,128]{3,2,1,0:T(4,128)(2,1)S(1)}, u32[]{:S(2)}, u32[]{:S(2)}) %all-to-all-start.3) | async-done | bytes 393248 | tf_op jit(solution)/shard_map/all_to_all | solution.py:411
  93.7 0.9 shard_map.117
  (7 shorter events, 0.0 us)
Async XLA Ops:
  0.6 30.0 %copy-start.4 = (bf16[128,128]{1,0:T(8,128)(2,1)S(1)}, bf16[128,128]{1,0:T(8,128)(2,1)}, u32[]{:S(2)}) copy-start(bf16[128,128]{1,0:T(8,128)(2,1)} %w_hbm.3) | copy-start | bytes 98308
  2.8 27.8 %all-to-all-start = ((bf16[128,24,128]{2,1,0:T(8,128)(2,1)}), bf16[128,24,128]{2,1,0:T(8,128)(2,1)S(1)}, u32[]{:S(2)}, u32[]{:S(2)}) async-start(bf16[128,24,128]{2,1,0:T(8,128)(2,1)} %shard_map.110), calls=%async_computation | async-start | bytes 1572864 | tf_op jit(solution)/shard_map/all_to_all | solution.py:336
  14.4 11.7 %collective-permute-start = (bf16[24,1024]{1,0:T(8,128)(2,1)}, bf16[24,1024]{1,0:T(8,128)(2,1)S(1)}, u32[]{:S(2)}, u32[]{:S(2)}) collective-permute-start(bf16[24,1024]{1,0:T(8,128)(2,1)} %seq_ref.3), channel_id=1, source_target_pairs={{0,0},{1,16},{2,32},{3,48},{4,64},{5,80},{6,96},{7,112},{8,1},{9,1... | collective-permute-start | bytes 147464 | tf_op jit(solution)/shard_map/ppermute | solution.py:335
  25.9 20.1 %copy-start = (f32[576,128]{1,0:T(8,128)S(1)}, f32[576,128]{1,0:T(8,128)}, u32[]{:S(2)}) copy-start(f32[576,128]{1,0:T(8,128)} %shard_map.111.rc_hbm) | copy-start | bytes 884740
  26.0 32.2 %copy-start.2 = (bf16[24,1024]{1,0:T(8,128)(2,1)S(1)}, bf16[24,1024]{1,0:T(8,128)(2,1)}, u32[]{:S(2)}) copy-start(bf16[24,1024]{1,0:T(8,128)(2,1)} %seq_ref.3) | copy-start | bytes 147460
  26.0 32.1 %copy-start.3 = (f32[1024]{0:T(1024)S(1)}, f32[1024]{0:T(1024)}, u32[]{:S(2)}) copy-start(f32[1024]{0:T(1024)} %param.8) | copy-start | bytes 12292
  26.0 32.1 %copy-start.5 = (f32[1024]{0:T(1024)S(1)}, f32[1024]{0:T(1024)}, u32[]{:S(2)}) copy-start(f32[1024]{0:T(1024)} %param.9) | copy-start | bytes 12292
  26.0 61.5 %copy-start.1 = (bf16[1024,128]{1,0:T(8,128)(2,1)S(1)}, bf16[1024,128]{1,0:T(8,128)(2,1)}, u32[]{:S(2)}) copy-start(bf16[1024,128]{1,0:T(8,128)(2,1)} %w_ref.1) | copy-start | bytes 786436
  39.9 18.2 %all-to-all-start.1 = ((bf16[128,3,4,128]{3,2,1,0:T(4,128)(2,1)}), bf16[128,3,4,128]{3,2,1,0:T(4,128)(2,1)S(1)}, u32[]{:S(2)}, u32[]{:S(2)}) async-start(bf16[128,3,4,128]{3,2,1,0:T(4,128)(2,1)} %get-tuple-element.18), calls=%async_computation.1 | async-start | bytes 786432 | tf_op jit(solution)/shard_map/all_to_all | solution.py:372
  76.8 16.9 %all-to-all-start.3 = ((bf16[128,3,4,128]{3,2,1,0:T(4,128)(2,1)}), bf16[128,3,4,128]{3,2,1,0:T(4,128)(2,1)S(1)}, u32[]{:S(2)}, u32[]{:S(2)}) async-start(bf16[128,3,4,128]{3,2,1,0:T(4,128)(2,1)} %get-tuple-element.26), calls=%async_computation.3 | async-start | bytes 786432 | tf_op jit(solution)/shard_map/all_to_all | solution.py:411
  81.7 5.8 %collective-permute-start.1 = (bf16[24,64]{1,0:T(8,128)(2,1)S(1)}, bf16[24,64]{1,0:T(8,128)(2,1)S(1)}, u32[]{:S(2)}, u32[]{:S(2)}) collective-permute-start(bf16[24,64]{1,0:T(8,128)(2,1)S(1)} %get-tuple-element.24), channel_id=1, source_target_pairs={{0,0},{16,1},{32,2},{48,3},{64,4},{80,5},{96,6},{112,7},{1,8},{17,... | collective-permute-start | bytes 9224 | tf_op jit(solution)/shard_map/ppermute | solution.py:402

commit v5 on v4

--- a/solution.py
+++ b/solution.py
@@ -269,16 +269,17 @@
     last = total[2]
     bo_ref[...] = last[1:2]
     bp_ref[...] = last[2:3] + last[3:4]
-    w_hi, w_lo = _split(last[0:1])
-    last = jnp.concatenate([w_hi, w_lo, jnp.zeros((2, last.shape[1]), F32)], axis=0)
-    tile = jnp.concatenate([total[:2], last[None]], axis=0).astype(BF16)
+    pairs = [total[at, row : row + 2] for at in (0, 1) for row in (0, 2)]
+    pairs.append(jnp.concatenate(_split(last[0:1]), axis=0))
+    tile = jnp.concatenate([p[None] for p in pairs], axis=0).astype(BF16)
     out_ref[...] = jnp.broadcast_to(tile[None], out_ref.shape)
 
 
 def _unpack_kernel(x_ref, w_proj_ref, w_out_ref):
     x = x_ref[...].astype(F32)
-    w_proj_ref[...] = jnp.concatenate([x[:, 0], x[:, 1]], axis=1).reshape(w_proj_ref.shape)
-    w_out_ref[...] = x[:, 2, 0] + x[:, 2, 1]
+    rows = jnp.concatenate([x[:, at] for at in range(4)], axis=1)
+    w_proj_ref[...] = rows.reshape(w_proj_ref.shape)
+    w_out_ref[...] = x[:, 4, 0] + x[:, 4, 1]
 
 
 def _seq_kernel(seq_ref, gain_ref, w_ref, dq_ref, dk_ref, out_ref):
@@ -403,7 +404,7 @@
 
     reduced, d_b_out, d_b_proj = pl.pallas_call(
         _reduce_kernel,
-        out_shape=(slot, shape((1, pair), F32), shape((1, pair), F32)),
+        out_shape=(shape((n, 5, 2, pair), BF16), shape((1, pair), F32), shape((1, pair), F32)),
         in_specs=[vmem],
         out_specs=(vmem,) * 3,
         compiler_params=_params(32),

time: 95 us -> 94.7 us (level)
  no operation moved by 1% of the time
where the time goes in v5:
time: 94.7 us; the launch traced here: 94.2 us
  starting transfers between devices  31.2 us (33%)
  Pallas kernels  30.5 us (32%)
  blocking collectives  16.9 us (18%)
  waiting for transfers between devices  14.7 us (16%)
    all_to_all x1, blocking collectives, local(): gathered = lax.all_to_all(slots, BOTH, 0, 0, tiled=True)  16.9 us
    all_to_all x1, starting transfers between devices, local(): qk_all = lax.all_to_all(qk, BOTH, 0, 0, tiled=True)  11.5 us
    pallas_call x1, Pallas kernels, local(): pl.pallas_call(functools.partial(_sums_kernel, nq, nk), out_shape=(slot,...  9.32 us
    pallas_call x1, Pallas kernels, local(): pl.pallas_call(_totals_kernel, out_shape=shape((rows + cols, pair), F32),...  7.91 us
    pallas_call x1, Pallas kernels, local(): pl.pallas_call(_weight_kernel, out_shape=(shape((pair, pair), F32), shape...  7.31 us
    all_to_all x1, starting transfers between devices, local(): dqk_in = lax.all_to_all(dqk_part, BOTH, 0, 0, tiled=True)  6.11 us
    ppermute x1, starting transfers between devices, local(): dk_own = lax.ppermute(dk_b, BOTH, to_owner)  5.05 us
    all_to_all x1, starting transfers between devices, local(): spread = lax.all_to_all(reduced, BOTH, 0, 0, tiled=True)  4.85 us
  transfers between devices with their start and end apart: 5, of which 4 were waited for; matrix products, arithmetic and copies ran while one was open for 0% of the time, Pallas kernels for 17%

profile of v5, /device:TPU:1, one launch (start us, length us, event | category | flops | bytes accessed | tf_op | source)
XLA Modules:
  0.0 94.2 jit_solution(10532041822766249014)
XLA Ops:
  0.6 2.2 %shard_map.110 = bf16[128,24,128]{2,1,0:T(8,128)(2,1)} custom-call(bf16[24,1024]{1,0:T(8,128)(2,1)} %seq_ref.3, f32[1,1024]{1,0:T(1,128)} %bitcast.5, f32[1,1024]{1,0:T(1,128)} %bitcast.8, bf16[1024,128]{1,0:T(8,128)(2,1)} %w_ref.1, f32[1,128]{1,0:T(1,128)} %bitcast.10), custom_call_target="tpu_custom_call" | custom-call | tf_op jit(solution)/shard_map/pallas_call | solution.py:317
  2.8 11.5 %all-to-all-start = ((bf16[128,24,128]{2,1,0:T(8,128)(2,1)}), bf16[128,24,128]{2,1,0:T(8,128)(2,1)S(1)}, u32[]{:S(2)}, u32[]{:S(2)}) async-start(bf16[128,24,128]{2,1,0:T(8,128)(2,1)} %shard_map.110), calls=%async_computation | async-start | bytes 1572864 | tf_op jit(solution)/shard_map/all_to_all | solution.py:337
  14.4 3.7 %collective-permute-start = (bf16[24,1024]{1,0:T(8,128)(2,1)}, bf16[24,1024]{1,0:T(8,128)(2,1)S(1)}, u32[]{:S(2)}, u32[]{:S(2)}) collective-permute-start(bf16[24,1024]{1,0:T(8,128)(2,1)} %seq_ref.3), channel_id=1, source_target_pairs={{0,0},{1,16},{2,32},{3,48},{4,64},{5,80},{6,96},{7,112},{8,1},{9,1... | collective-permute-start | bytes 147464 | tf_op jit(solution)/shard_map/ppermute | solution.py:336
  18.0 7.9 %shard_map.111.rc_hbm = f32[576,128]{1,0:T(8,128)} custom-call(bf16[384,192,128]{2,1,0:T(8,128)(2,1)} %pg_hbm.5), custom_call_target="tpu_custom_call" | custom-call | flops 4831838208 | bytes 28311552 | tf_op jit(solution)/shard_map/pallas_call | solution.py:339
  26.0 0.0 copy-start.2
  26.0 0.0 copy-start.3
  26.0 0.0 copy-start.5
  26.0 0.0 copy-start.1
  26.0 0.0 collective-permute-done.seqk_hbm.seqk_ref
  26.0 4.6 %all-to-all-done.qk_hbm = bf16[128,24,128]{2,1,0:T(8,128)(2,1)S(1)} async-done(((bf16[128,24,128]{2,1,0:T(8,128)(2,1)}), bf16[128,24,128]{2,1,0:T(8,128)(2,1)S(1)}, u32[]{:S(2)}, u32[]{:S(2)}) %all-to-all-start) | async-done | bytes 786464 | tf_op jit(solution)/shard_map/all_to_all | solution.py:337
  30.6 9.3 %shard_map.112 = (bf16[128,3,4,128]{3,2,1,0:T(4,128)(2,1)}, f32[24,64]{1,0:T(8,128)S(1)}, f32[1,128]{1,0:T(1,128)S(1)}) custom-call(bf16[128,24,128]{2,1,0:T(8,128)(2,1)S(1)} %all-to-all-done.qk_hbm, f32[576,128]{1,0:T(8,128)} %shard_map.111.rc_hbm, bf16[128,128]{1,0:T(8,128)(2,1)S(1)} %copy-done.4, bf16[384,192,128]{2,1,0:T(8,128)(2,1)} %pg_hbm.5, ...), custom_call_target="tpu_custom_call" | custom-call | tf_op jit(solution)/shard_map/pallas_call | solution.py:353
  39.9 6.1 %all-to-all-start.1 = ((bf16[128,3,4,128]{3,2,1,0:T(4,128)(2,1)}), bf16[128,3,4,128]{3,2,1,0:T(4,128)(2,1)S(1)}, u32[]{:S(2)}, u32[]{:S(2)}) async-start(bf16[128,3,4,128]{3,2,1,0:T(4,128)(2,1)} %get-tuple-element.18), calls=%async_computation.1 | async-start | bytes 786432 | tf_op jit(solution)/shard_map/all_to_all | solution.py:373
  46.1 0.0 copy-done
  46.1 7.3 %shard_map.113 = (f32[128,128]{1,0:T(8,128)S(1)}, f32[1,128]{1,0:T(1,128)S(1)}) custom-call(bf16[128,24,128]{2,1,0:T(8,128)(2,1)S(1)} %all-to-all-done.qk_hbm, f32[576,128]{1,0:T(8,128)S(1)} %copy-done, bf16[384,192,128]{2,1,0:T(8,128)(2,1)} %pg_hbm.5), custom_call_target="tpu_custom_call" | custom-call | flops 4831838208 | bytes 18874368 | tf_op jit(solution)/shard_map/pallas_call | solution.py:375
  53.4 4.7 %all-to-all-done.1.dqk_ref = bf16[128,3,4,128]{3,2,1,0:T(4,128)(2,1)S(1)} async-done(((bf16[128,3,4,128]{3,2,1,0:T(4,128)(2,1)}), bf16[128,3,4,128]{3,2,1,0:T(4,128)(2,1)S(1)}, u32[]{:S(2)}, u32[]{:S(2)}) %all-to-all-start.1) | async-done | bytes 393248 | tf_op jit(solution)/shard_map/all_to_all | solution.py:373
  58.1 0.7 shard_map.114
  58.9 16.9 %all_to_all.20.x_ref = bf16[128,3,4,128]{3,2,1,0:T(4,128)(2,1)S(1)} all-to-all(bf16[128,3,4,128]{3,2,1,0:T(4,128)(2,1)S(1)} %get-tuple-element.25), channel_id=1, replica_groups=mesh['row'=8,'col'=16] {'row','col'}, dimensions={0} | all-to-all | bytes 786432 | tf_op jit(solution)/shard_map/all_to_all | solution.py:402
  75.8 1.1 %shard_map.116 = (bf16[128,5,2,128]{3,2,1,0:T(2,128)(2,1)}, f32[1,128]{1,0:T(1,128)}, f32[1,128]{1,0:T(1,128)}) custom-call(bf16[128,3,4,128]{3,2,1,0:T(4,128)(2,1)S(1)} %all_to_all.20.x_ref), custom_call_target="tpu_custom_call" | custom-call | tf_op jit(solution)/shard_map/pallas_call | solution.py:405
  76.9 4.8 %all-to-all-start.3 = ((bf16[128,5,2,128]{3,2,1,0:T(2,128)(2,1)}), bf16[128,5,2,128]{3,2,1,0:T(2,128)(2,1)S(1)}, u32[]{:S(2)}, u32[]{:S(2)}) async-start(bf16[128,5,2,128]{3,2,1,0:T(2,128)(2,1)} %get-tuple-element.26), calls=%async_computation.3 | async-start | bytes 655360 | tf_op jit(solution)/shard_map/all_to_all | solution.py:412
  81.7 5.1 %collective-permute-start.1 = (bf16[24,64]{1,0:T(8,128)(2,1)S(1)}, bf16[24,64]{1,0:T(8,128)(2,1)S(1)}, u32[]{:S(2)}, u32[]{:S(2)}) collective-permute-start(bf16[24,64]{1,0:T(8,128)(2,1)S(1)} %get-tuple-element.24), channel_id=1, source_target_pairs={{0,0},{16,1},{32,2},{48,3},{64,4},{80,5},{96,6},{112,7},{1,8},{17,... | collective-permute-start | bytes 9224 | tf_op jit(solution)/shard_map/ppermute | solution.py:403
  86.8 0.8 collective-permute-done.1.dk_ref
  87.5 0.9 %shard_map.115 = bf16[24,1024]{1,0:T(8,128)(2,1)} custom-call(bf16[24,1024]{1,0:T(8,128)(2,1)S(1)} %copy-done.2, f32[1,1024]{1,0:T(1,128)S(1)} %bitcast.7, bf16[1024,128]{1,0:T(8,128)(2,1)S(1)} %copy-done.1, bf16[24,64]{1,0:T(8,128)(2,1)S(1)} %get-tuple-element.23.dq_ref, bf16[24,64]{1,0:T(8,128)(2,1)S(1)} %collective-permute-done.1.dk_ref), custom_call_target="tpu_custom_call" | custom-call | tf_op jit(solution)/shard_map/pallas_call | solution.py:414
  88.5 4.6 %all-to-all-done.3.x_ref = bf16[128,5,2,128]{3,2,1,0:T(2,128)(2,1)S(1)} async-done(((bf16[128,5,2,128]{3,2,1,0:T(2,128)(2,1)}), bf16[128,5,2,128]{3,2,1,0:T(2,128)(2,1)S(1)}, u32[]{:S(2)}, u32[]{:S(2)}) %all-to-all-start.3) | async-done | bytes 327712 | tf_op jit(solution)/shard_map/all_to_all | solution.py:412
  93.1 1.0 %shard_map.117 = (f32[1024,128]{1,0:T(8,128)}, f32[128,128]{1,0:T(8,128)}) custom-call(bf16[128,5,2,128]{3,2,1,0:T(2,128)(2,1)S(1)} %all-to-all-done.3.x_ref), custom_call_target="tpu_custom_call" | custom-call | tf_op jit(solution)/shard_map/pallas_call | solution.py:422
  (7 shorter events, 0.0 us)
Async XLA Ops:
  0.6 30.0 %copy-start.4 = (bf16[128,128]{1,0:T(8,128)(2,1)S(1)}, bf16[128,128]{1,0:T(8,128)(2,1)}, u32[]{:S(2)}) copy-start(bf16[128,128]{1,0:T(8,128)(2,1)} %w_hbm.3) | copy-start | bytes 98308
  2.8 27.8 %all-to-all-start = ((bf16[128,24,128]{2,1,0:T(8,128)(2,1)}), bf16[128,24,128]{2,1,0:T(8,128)(2,1)S(1)}, u32[]{:S(2)}, u32[]{:S(2)}) async-start(bf16[128,24,128]{2,1,0:T(8,128)(2,1)} %shard_map.110), calls=%async_computation | async-start | bytes 1572864 | tf_op jit(solution)/shard_map/all_to_all | solution.py:337
  14.4 11.7 %collective-permute-start = (bf16[24,1024]{1,0:T(8,128)(2,1)}, bf16[24,1024]{1,0:T(8,128)(2,1)S(1)}, u32[]{:S(2)}, u32[]{:S(2)}) collective-permute-start(bf16[24,1024]{1,0:T(8,128)(2,1)} %seq_ref.3), channel_id=1, source_target_pairs={{0,0},{1,16},{2,32},{3,48},{4,64},{5,80},{6,96},{7,112},{8,1},{9,1... | collective-permute-start | bytes 147464 | tf_op jit(solution)/shard_map/ppermute | solution.py:336
  25.9 20.1 %copy-start = (f32[576,128]{1,0:T(8,128)S(1)}, f32[576,128]{1,0:T(8,128)}, u32[]{:S(2)}) copy-start(f32[576,128]{1,0:T(8,128)} %shard_map.111.rc_hbm) | copy-start | bytes 884740
  26.0 32.2 %copy-start.2 = (bf16[24,1024]{1,0:T(8,128)(2,1)S(1)}, bf16[24,1024]{1,0:T(8,128)(2,1)}, u32[]{:S(2)}) copy-start(bf16[24,1024]{1,0:T(8,128)(2,1)} %seq_ref.3) | copy-start | bytes 147460
  26.0 32.1 %copy-start.3 = (f32[1024]{0:T(1024)S(1)}, f32[1024]{0:T(1024)}, u32[]{:S(2)}) copy-start(f32[1024]{0:T(1024)} %param.8) | copy-start | bytes 12292
  26.0 32.1 %copy-start.5 = (f32[1024]{0:T(1024)S(1)}, f32[1024]{0:T(1024)}, u32[]{:S(2)}) copy-start(f32[1024]{0:T(1024)} %param.9) | copy-start | bytes 12292
  26.0 61.5 %copy-start.1 = (bf16[1024,128]{1,0:T(8,128)(2,1)S(1)}, bf16[1024,128]{1,0:T(8,128)(2,1)}, u32[]{:S(2)}) copy-start(bf16[1024,128]{1,0:T(8,128)(2,1)} %w_ref.1) | copy-start | bytes 786436
  39.9 18.2 %all-to-all-start.1 = ((bf16[128,3,4,128]{3,2,1,0:T(4,128)(2,1)}), bf16[128,3,4,128]{3,2,1,0:T(4,128)(2,1)S(1)}, u32[]{:S(2)}, u32[]{:S(2)}) async-start(bf16[128,3,4,128]{3,2,1,0:T(4,128)(2,1)} %get-tuple-element.18), calls=%async_computation.1 | async-start | bytes 786432 | tf_op jit(solution)/shard_map/all_to_all | solution.py:373
  76.9 16.3 %all-to-all-start.3 = ((bf16[128,5,2,128]{3,2,1,0:T(2,128)(2,1)}), bf16[128,5,2,128]{3,2,1,0:T(2,128)(2,1)S(1)}, u32[]{:S(2)}, u32[]{:S(2)}) async-start(bf16[128,5,2,128]{3,2,1,0:T(2,128)(2,1)} %get-tuple-element.26), calls=%async_computation.3 | async-start | bytes 655360 | tf_op jit(solution)/shard_map/all_to_all | solution.py:412
  81.7 5.8 %collective-permute-start.1 = (bf16[24,64]{1,0:T(8,128)(2,1)S(1)}, bf16[24,64]{1,0:T(8,128)(2,1)S(1)}, u32[]{:S(2)}, u32[]{:S(2)}) collective-permute-start(bf16[24,64]{1,0:T(8,128)(2,1)S(1)} %get-tuple-element.24), channel_id=1, source_target_pairs={{0,0},{16,1},{32,2},{48,3},{64,4},{80,5},{96,6},{112,7},{1,8},{17,... | collective-permute-start | bytes 9224 | tf_op jit(solution)/shard_map/ppermute | solution.py:403

commit v6 on v5

--- a/solution.py
+++ b/solution.py
@@ -264,7 +264,7 @@
     out_ref[:, 2] = last.astype(BF16)
 
 
-def _reduce_kernel(x_ref, out_ref, bo_ref, bp_ref):
+def _reduce_kernel(x_ref, out_hbm, bo_ref, bp_ref, block_s, out_sems):
     total = jnp.sum(x_ref[...].astype(F32), axis=0)
     last = total[2]
     bo_ref[...] = last[1:2]
@@ -272,7 +272,8 @@
     pairs = [total[at, row : row + 2] for at in (0, 1) for row in (0, 2)]
     pairs.append(jnp.concatenate(_split(last[0:1]), axis=0))
     tile = jnp.concatenate([p[None] for p in pairs], axis=0).astype(BF16)
-    out_ref[...] = jnp.broadcast_to(tile[None], out_ref.shape)
+    block_s[...] = jnp.broadcast_to(tile[None], block_s.shape)
+    _spread(block_s, out_hbm, out_sems)
 
 
 def _unpack_kernel(x_ref, w_proj_ref, w_out_ref):
@@ -406,7 +407,11 @@
         _reduce_kernel,
         out_shape=(shape((n, 5, 2, pair), BF16), shape((1, pair), F32), shape((1, pair), F32)),
         in_specs=[vmem],
-        out_specs=(vmem,) * 3,
+        out_specs=(hbm, vmem, vmem),
+        scratch_shapes=[
+            pltpu.VMEM((n // 8, 5, 2, pair), BF16),
+            pltpu.SemaphoreType.DMA((8,)),
+        ],
         compiler_params=_params(32),
     )(gathered)
     spread = lax.all_to_all(reduced, BOTH, 0, 0, tiled=True)

time: 94.7 us -> 95.1 us (level)
  no operation moved by 1% of the time
where the time goes in v6:
time: 95.1 us; the launch traced here: 94.6 us
  starting transfers between devices  31.2 us (33%)
  Pallas kernels  31 us (33%)
  blocking collectives  16.9 us (18%)
  waiting for transfers between devices  14.7 us (15%)
    all_to_all x1, blocking collectives, local(): gathered = lax.all_to_all(slots, BOTH, 0, 0, tiled=True)  16.9 us
    all_to_all x1, starting transfers between devices, local(): qk_all = lax.all_to_all(qk, BOTH, 0, 0, tiled=True)  11.5 us
    pallas_call x1, Pallas kernels, local(): pl.pallas_call(functools.partial(_sums_kernel, nq, nk), out_shape=(slot,...  9.32 us
    pallas_call x1, Pallas kernels, local(): pl.pallas_call(_totals_kernel, out_shape=shape((rows + cols, pair), F32),...  7.91 us
    pallas_call x1, Pallas kernels, local(): pl.pallas_call(_weight_kernel, out_shape=(shape((pair, pair), F32), shape...  7.31 us
    all_to_all x1, starting transfers between devices, local(): dqk_in = lax.all_to_all(dqk_part, BOTH, 0, 0, tiled=True)  6.11 us
    ppermute x1, starting transfers between devices, local(): dk_own = lax.ppermute(dk_b, BOTH, to_owner)  5.05 us
    all_to_all x1, starting transfers between devices, local(): spread = lax.all_to_all(reduced, BOTH, 0, 0, tiled=True)  4.85 us
  transfers between devices with their start and end apart: 5, of which 4 were waited for; matrix products, arithmetic and copies ran while one was open for 0% of the time, Pallas kernels for 17%

profile of v6, /device:TPU:1, one launch (start us, length us, event | category | flops | bytes accessed | tf_op | source)
XLA Modules:
  0.0 94.6 jit_solution(2247889515465558302)
XLA Ops:
  0.6 2.2 %shard_map.110 = bf16[128,24,128]{2,1,0:T(8,128)(2,1)} custom-call(bf16[24,1024]{1,0:T(8,128)(2,1)} %seq_ref.3, f32[1,1024]{1,0:T(1,128)} %bitcast.5, f32[1,1024]{1,0:T(1,128)} %bitcast.8, bf16[1024,128]{1,0:T(8,128)(2,1)} %w_ref.1, f32[1,128]{1,0:T(1,128)} %bitcast.10), custom_call_target="tpu_custom_call" | custom-call | tf_op jit(solution)/shard_map/pallas_call | solution.py:318
  2.8 11.5 %all-to-all-start = ((bf16[128,24,128]{2,1,0:T(8,128)(2,1)}), bf16[128,24,128]{2,1,0:T(8,128)(2,1)S(1)}, u32[]{:S(2)}, u32[]{:S(2)}) async-start(bf16[128,24,128]{2,1,0:T(8,128)(2,1)} %shard_map.110), calls=%async_computation | async-start | bytes 1572864 | tf_op jit(solution)/shard_map/all_to_all | solution.py:338
  14.4 3.7 %collective-permute-start = (bf16[24,1024]{1,0:T(8,128)(2,1)}, bf16[24,1024]{1,0:T(8,128)(2,1)S(1)}, u32[]{:S(2)}, u32[]{:S(2)}) collective-permute-start(bf16[24,1024]{1,0:T(8,128)(2,1)} %seq_ref.3), channel_id=1, source_target_pairs={{0,0},{1,16},{2,32},{3,48},{4,64},{5,80},{6,96},{7,112},{8,1},{9,1... | collective-permute-start | bytes 147464 | tf_op jit(solution)/shard_map/ppermute | solution.py:337
  18.0 7.9 %shard_map.111.rc_hbm = f32[576,128]{1,0:T(8,128)} custom-call(bf16[384,192,128]{2,1,0:T(8,128)(2,1)} %pg_hbm.5), custom_call_target="tpu_custom_call" | custom-call | flops 4831838208 | bytes 28311552 | tf_op jit(solution)/shard_map/pallas_call | solution.py:340
  26.0 0.0 copy-start.2
  26.0 0.0 copy-start.3
  26.0 0.0 copy-start.5
  26.0 0.0 copy-start.1
  26.0 0.0 collective-permute-done.seqk_hbm.seqk_ref
  26.0 4.6 %all-to-all-done.qk_hbm = bf16[128,24,128]{2,1,0:T(8,128)(2,1)S(1)} async-done(((bf16[128,24,128]{2,1,0:T(8,128)(2,1)}), bf16[128,24,128]{2,1,0:T(8,128)(2,1)S(1)}, u32[]{:S(2)}, u32[]{:S(2)}) %all-to-all-start) | async-done | bytes 786464 | tf_op jit(solution)/shard_map/all_to_all | solution.py:338
  30.6 0.0 copy-done.4
  30.6 9.3 %shard_map.112 = (bf16[128,3,4,128]{3,2,1,0:T(4,128)(2,1)}, f32[24,64]{1,0:T(8,128)S(1)}, f32[1,128]{1,0:T(1,128)S(1)}) custom-call(bf16[128,24,128]{2,1,0:T(8,128)(2,1)S(1)} %all-to-all-done.qk_hbm, f32[576,128]{1,0:T(8,128)} %shard_map.111.rc_hbm, bf16[128,128]{1,0:T(8,128)(2,1)S(1)} %copy-done.4, bf16[384,192,128]{2,1,0:T(8,128)(2,1)} %pg_hbm.5, ...), custom_call_target="tpu_custom_call" | custom-call | tf_op jit(solution)/shard_map/pallas_call | solution.py:354
  39.9 6.1 %all-to-all-start.1 = ((bf16[128,3,4,128]{3,2,1,0:T(4,128)(2,1)}), bf16[128,3,4,128]{3,2,1,0:T(4,128)(2,1)S(1)}, u32[]{:S(2)}, u32[]{:S(2)}) async-start(bf16[128,3,4,128]{3,2,1,0:T(4,128)(2,1)} %get-tuple-element.18), calls=%async_computation.1 | async-start | bytes 786432 | tf_op jit(solution)/shard_map/all_to_all | solution.py:374
  46.1 7.3 %shard_map.113 = (f32[128,128]{1,0:T(8,128)S(1)}, f32[1,128]{1,0:T(1,128)S(1)}) custom-call(bf16[128,24,128]{2,1,0:T(8,128)(2,1)S(1)} %all-to-all-done.qk_hbm, f32[576,128]{1,0:T(8,128)S(1)} %copy-done, bf16[384,192,128]{2,1,0:T(8,128)(2,1)} %pg_hbm.5), custom_call_target="tpu_custom_call" | custom-call | flops 4831838208 | bytes 18874368 | tf_op jit(solution)/shard_map/pallas_call | solution.py:376
  53.4 4.7 %all-to-all-done.1.dqk_ref = bf16[128,3,4,128]{3,2,1,0:T(4,128)(2,1)S(1)} async-done(((bf16[128,3,4,128]{3,2,1,0:T(4,128)(2,1)}), bf16[128,3,4,128]{3,2,1,0:T(4,128)(2,1)S(1)}, u32[]{:S(2)}, u32[]{:S(2)}) %all-to-all-start.1) | async-done | bytes 393248 | tf_op jit(solution)/shard_map/all_to_all | solution.py:374
  58.1 0.7 shard_map.114
  58.9 16.9 %all_to_all.20.x_ref = bf16[128,3,4,128]{3,2,1,0:T(4,128)(2,1)S(1)} all-to-all(bf16[128,3,4,128]{3,2,1,0:T(4,128)(2,1)S(1)} %get-tuple-element.25), channel_id=1, replica_groups=mesh['row'=8,'col'=16] {'row','col'}, dimensions={0} | all-to-all | bytes 786432 | tf_op jit(solution)/shard_map/all_to_all | solution.py:403
  75.8 1.5 %shard_map.116 = (bf16[128,5,2,128]{3,2,1,0:T(2,128)(2,1)}, f32[1,128]{1,0:T(1,128)}, f32[1,128]{1,0:T(1,128)}) custom-call(bf16[128,3,4,128]{3,2,1,0:T(4,128)(2,1)S(1)} %all_to_all.20.x_ref), custom_call_target="tpu_custom_call" | custom-call | tf_op jit(solution)/shard_map/pallas_call | solution.py:406
  77.3 4.9 %all-to-all-start.3 = ((bf16[128,5,2,128]{3,2,1,0:T(2,128)(2,1)}), bf16[128,5,2,128]{3,2,1,0:T(2,128)(2,1)S(1)}, u32[]{:S(2)}, u32[]{:S(2)}) async-start(bf16[128,5,2,128]{3,2,1,0:T(2,128)(2,1)} %get-tuple-element.26), calls=%async_computation.3 | async-start | bytes 655360 | tf_op jit(solution)/shard_map/all_to_all | solution.py:417
  82.2 5.1 %collective-permute-start.1 = (bf16[24,64]{1,0:T(8,128)(2,1)S(1)}, bf16[24,64]{1,0:T(8,128)(2,1)S(1)}, u32[]{:S(2)}, u32[]{:S(2)}) collective-permute-start(bf16[24,64]{1,0:T(8,128)(2,1)S(1)} %get-tuple-element.24), channel_id=1, source_target_pairs={{0,0},{16,1},{32,2},{48,3},{64,4},{80,5},{96,6},{112,7},{1,8},{17,... | collective-permute-start | bytes 9224 | tf_op jit(solution)/shard_map/ppermute | solution.py:404
  87.2 0.8 collective-permute-done.1.dk_ref
  88.0 0.9 shard_map.115
  88.9 4.6 %all-to-all-done.3.x_ref = bf16[128,5,2,128]{3,2,1,0:T(2,128)(2,1)S(1)} async-done(((bf16[128,5,2,128]{3,2,1,0:T(2,128)(2,1)}), bf16[128,5,2,128]{3,2,1,0:T(2,128)(2,1)S(1)}, u32[]{:S(2)}, u32[]{:S(2)}) %all-to-all-start.3) | async-done | bytes 327712 | tf_op jit(solution)/shard_map/all_to_all | solution.py:417
  93.6 1.0 %shard_map.117 = (f32[1024,128]{1,0:T(8,128)}, f32[128,128]{1,0:T(8,128)}) custom-call(bf16[128,5,2,128]{3,2,1,0:T(2,128)(2,1)S(1)} %all-to-all-done.3.x_ref), custom_call_target="tpu_custom_call" | custom-call | tf_op jit(solution)/shard_map/pallas_call | solution.py:427
  (7 shorter events, 0.0 us)
Async XLA Ops:
  0.6 30.0 %copy-start.4 = (bf16[128,128]{1,0:T(8,128)(2,1)S(1)}, bf16[128,128]{1,0:T(8,128)(2,1)}, u32[]{:S(2)}) copy-start(bf16[128,128]{1,0:T(8,128)(2,1)} %w_hbm.3) | copy-start | bytes 98308
  2.8 27.8 %all-to-all-start = ((bf16[128,24,128]{2,1,0:T(8,128)(2,1)}), bf16[128,24,128]{2,1,0:T(8,128)(2,1)S(1)}, u32[]{:S(2)}, u32[]{:S(2)}) async-start(bf16[128,24,128]{2,1,0:T(8,128)(2,1)} %shard_map.110), calls=%async_computation | async-start | bytes 1572864 | tf_op jit(solution)/shard_map/all_to_all | solution.py:338
  14.4 11.7 %collective-permute-start = (bf16[24,1024]{1,0:T(8,128)(2,1)}, bf16[24,1024]{1,0:T(8,128)(2,1)S(1)}, u32[]{:S(2)}, u32[]{:S(2)}) collective-permute-start(bf16[24,1024]{1,0:T(8,128)(2,1)} %seq_ref.3), channel_id=1, source_target_pairs={{0,0},{1,16},{2,32},{3,48},{4,64},{5,80},{6,96},{7,112},{8,1},{9,1... | collective-permute-start | bytes 147464 | tf_op jit(solution)/shard_map/ppermute | solution.py:337
  25.9 20.1 %copy-start = (f32[576,128]{1,0:T(8,128)S(1)}, f32[576,128]{1,0:T(8,128)}, u32[]{:S(2)}) copy-start(f32[576,128]{1,0:T(8,128)} %shard_map.111.rc_hbm) | copy-start | bytes 884740
  26.0 32.2 %copy-start.2 = (bf16[24,1024]{1,0:T(8,128)(2,1)S(1)}, bf16[24,1024]{1,0:T(8,128)(2,1)}, u32[]{:S(2)}) copy-start(bf16[24,1024]{1,0:T(8,128)(2,1)} %seq_ref.3) | copy-start | bytes 147460
  26.0 32.1 %copy-start.3 = (f32[1024]{0:T(1024)S(1)}, f32[1024]{0:T(1024)}, u32[]{:S(2)}) copy-start(f32[1024]{0:T(1024)} %param.8) | copy-start | bytes 12292
  26.0 32.1 %copy-start.5 = (f32[1024]{0:T(1024)S(1)}, f32[1024]{0:T(1024)}, u32[]{:S(2)}) copy-start(f32[1024]{0:T(1024)} %param.9) | copy-start | bytes 12292
  26.0 62.0 %copy-start.1 = (bf16[1024,128]{1,0:T(8,128)(2,1)S(1)}, bf16[1024,128]{1,0:T(8,128)(2,1)}, u32[]{:S(2)}) copy-start(bf16[1024,128]{1,0:T(8,128)(2,1)} %w_ref.1) | copy-start | bytes 786436
  39.9 18.2 %all-to-all-start.1 = ((bf16[128,3,4,128]{3,2,1,0:T(4,128)(2,1)}), bf16[128,3,4,128]{3,2,1,0:T(4,128)(2,1)S(1)}, u32[]{:S(2)}, u32[]{:S(2)}) async-start(bf16[128,3,4,128]{3,2,1,0:T(4,128)(2,1)} %get-tuple-element.18), calls=%async_computation.1 | async-start | bytes 786432 | tf_op jit(solution)/shard_map/all_to_all | solution.py:374
  77.3 16.3 %all-to-all-start.3 = ((bf16[128,5,2,128]{3,2,1,0:T(2,128)(2,1)}), bf16[128,5,2,128]{3,2,1,0:T(2,128)(2,1)S(1)}, u32[]{:S(2)}, u32[]{:S(2)}) async-start(bf16[128,5,2,128]{3,2,1,0:T(2,128)(2,1)} %get-tuple-element.26), calls=%async_computation.3 | async-start | bytes 655360 | tf_op jit(solution)/shard_map/all_to_all | solution.py:417
  82.2 5.8 %collective-permute-start.1 = (bf16[24,64]{1,0:T(8,128)(2,1)S(1)}, bf16[24,64]{1,0:T(8,128)(2,1)S(1)}, u32[]{:S(2)}, u32[]{:S(2)}) collective-permute-start(bf16[24,64]{1,0:T(8,128)(2,1)S(1)} %get-tuple-element.24), channel_id=1, source_target_pairs={{0,0},{16,1},{32,2},{48,3},{64,4},{80,5},{96,6},{112,7},{1,8},{17,... | collective-permute-start | bytes 9224 | tf_op jit(solution)/shard_map/ppermute | solution.py:404
